TPU v7x, 256 devices: a whole 4x4x8 slice. The times are simulated.
256 devices in a mesh: member: 8 (over z_lo, core), space: 32 (over z_hi, x, y).
Axes of the slice: x: 4, y: 4, z: 8 (z_hi: 2, z_lo: 4; z = z_hi * 4 + z_lo), core: 2. Of those that a mesh axis runs over, the one named last changes fastest.
Arguments:
- ensemble: bfloat16 [8, 512, 64, 256], P('member', 'space'), may hold values from -6 to 6
- shifts: int32 [2], replicated, may hold values from 0 to 15
- land_sea: int32 [512, 64], replicated, may hold values 0 or 1
- member_gain: float32 [256], replicated, may hold values from 0.25 to 1.75
- member_qkv: bfloat16 [256, 768], replicated, may hold values from -0.375 to 0.375
- member_out: bfloat16 [256, 256], replicated, may hold values from -0.375 to 0.375
- first_gain: float32 [256], replicated, may hold values from 0.25 to 1.75
- first_in: bfloat16 [256, 1024], replicated, may hold values from -0.375 to 0.375
- first_out: bfloat16 [1024, 256], replicated, may hold values from -0.1875 to 0.1875
- window_gain: float32 [256], replicated, may hold values from 0.25 to 1.75
- window_qkv: bfloat16 [256, 768], replicated, may hold values from -0.375 to 0.375
- window_out: bfloat16 [256, 256], replicated, may hold values from -0.375 to 0.375
- second_gain: float32 [256], replicated, may hold values from 0.25 to 1.75
- second_in: bfloat16 [256, 1024], replicated, may hold values from -0.375 to 0.375
- second_out: bfloat16 [1024, 256], replicated, may hold values from -0.1875 to 0.1875
Outputs:
- processed: bfloat16 [8, 512, 64, 256], P('member', 'space')
Inputs may be any that keep to these rules, and one draw needn't show every extreme that they name: `land_sea`: 1 marks land, 0 sea.
All inputs are finite; a program needn't handle non-finite values.
Results may differ from a plain program's by a relative error of at most 0.015.
Values may be sent and summed in bfloat16 or wider, within the bound.
No kernel may reach another device: no remote copies, remote signals or barrier semaphores. Data moves between devices by JAX's collectives and lax.ppermute only.
A program may use at most 128 MiB of HBM per device.

v0:
```python
import math

import jax
import jax.numpy as jnp
from jax import lax
from jax.sharding import PartitionSpec as P

HEADS = 8
WIN = 16


EPSILON = 1e-05


def padded(shard, sides, width):
    for axis, dim in sides:
        devices, length = (lax.axis_size(axis), shard.shape[dim])
        up = [(i, (i + 1) % devices) for i in range(devices)]
        down = [(j, i) for i, j in up]
        last = lax.slice_in_dim(shard, length - width, length, axis=dim)
        leading = lax.slice_in_dim(shard, 0, width, axis=dim)
        before = lax.ppermute(last, axis, up)
        after = lax.ppermute(leading, axis, down)
        shard = jnp.concatenate([before, shard, after], axis=dim)
    return shard


def layer_norm(values, gains):
    values = values.astype(jnp.float32)
    center = jnp.mean(values, axis=-1, keepdims=True)
    spread = jnp.mean(jnp.square(values - center), axis=-1, keepdims=True)
    return ((values - center) * lax.rsqrt(spread + EPSILON) * gains).astype(jnp.bfloat16)


def attend(normed, w_qkv, w_out, allowed):
    groups, length, features = normed.shape
    head_size = features // HEADS
    projected = jnp.dot(normed.reshape(-1, features), w_qkv, preferred_element_type=jnp.float32)
    projected = projected.astype(jnp.bfloat16).reshape(groups, length, 3, HEADS, head_size)
    scores = jnp.einsum(
        "bqhd,bkhd->bhqk",
        projected[:, :, 0],
        projected[:, :, 1],
        preferred_element_type=jnp.float32,
    ) / math.sqrt(head_size)
    if allowed is not None:
        scores = jnp.where(allowed[:, None], scores, -1e30)
    weights = jax.nn.softmax(scores, axis=-1).astype(jnp.bfloat16)
    attended = jnp.einsum(
        "bhqk,bkhd->bqhd", weights, projected[:, :, 2], preferred_element_type=jnp.float32
    ).astype(jnp.bfloat16)
    result = jnp.dot(attended.reshape(-1, features), w_out, preferred_element_type=jnp.float32)
    return result.reshape(groups, length, features)


def feed_forward(stream, gains, w_in, w_out):
    features = stream.shape[-1]
    normed = layer_norm(stream, gains).reshape(-1, features)
    hidden = jax.nn.gelu(jnp.dot(normed, w_in, preferred_element_type=jnp.float32)).astype(
        jnp.bfloat16
    )
    update = jnp.dot(hidden, w_out, preferred_element_type=jnp.float32).reshape(stream.shape)
    return (stream.astype(jnp.float32) + update).astype(jnp.bfloat16)


def window_layer(region, surface_kinds, gains, w_qkv, w_out):
    mem_dev, row_count, longitudes, features = region.shape
    tokens_in = region.reshape(
        mem_dev, row_count // WIN, WIN, longitudes // WIN, WIN, features
    ).transpose(0, 1, 3, 2, 4, 5)
    tokens_in = tokens_in.reshape(-1, WIN * WIN, features)
    flat_kinds = (
        surface_kinds.reshape(row_count // WIN, WIN, longitudes // WIN, WIN)
        .transpose(0, 2, 1, 3)
        .reshape(-1, WIN * WIN)
    )
    allowed = flat_kinds[:, :, None] == flat_kinds[:, None, :]
    allowed = jnp.tile(allowed, (mem_dev, 1, 1))
    attended = attend(layer_norm(tokens_in, gains), w_qkv, w_out, allowed)
    stream = (tokens_in.astype(jnp.float32) + attended).astype(jnp.bfloat16)
    stream = stream.reshape(
        mem_dev, row_count // WIN, longitudes // WIN, WIN, WIN, features
    ).transpose(0, 1, 3, 2, 4, 5)
    return stream.reshape(mem_dev, row_count, longitudes, features)


def on_device(
    ensemble,
    shifts,
    land_sea,
    member_gain,
    member_qkv,
    member_out,
    first_gain,
    first_in,
    first_out,
    window_gain,
    window_qkv,
    window_out,
    second_gain,
    second_in,
    second_out,
):
    mem_dev, rows_dev, longitudes, features = ensemble.shape
    points_dev = rows_dev * longitudes
    flattened = ensemble.reshape(mem_dev, points_dev, features)
    member_count = lax.axis_size("member")
    grouped = flattened.reshape(mem_dev, member_count, points_dev // member_count, features)
    points = jnp.swapaxes(
        lax.all_to_all(grouped, "member", split_axis=1, concat_axis=0, tiled=True)[:, 0], 0, 1
    )
    attended = attend(layer_norm(points, member_gain), member_qkv, member_out, None)
    stream_here = (points.astype(jnp.float32) + attended).astype(jnp.bfloat16)
    stream_here = feed_forward(stream_here, first_gain, first_in, first_out)
    mixed_points = jnp.swapaxes(stream_here, 0, 1)[:, None]
    returned = lax.all_to_all(mixed_points, "member", split_axis=0, concat_axis=1, tiled=True)
    stream = returned.reshape(mem_dev, points_dev, features)
    lat_shift = shifts[0]
    lon_shift = shifts[1]
    gridded = jnp.roll(stream.reshape(mem_dev, rows_dev, longitudes, features), -lon_shift, axis=2)
    total_rows = rows_dev * lax.axis_size("space")
    first_row = lax.axis_index("space") * rows_dev
    widened = padded(gridded, (("space", 1),), WIN)
    region = lax.dynamic_slice_in_dim(widened, lat_shift, rows_dev + WIN, 1)
    row_index = (
        first_row - WIN + lat_shift + jnp.arange(rows_dev + WIN, dtype=jnp.int32)
    ) % total_rows
    picked = jnp.take(land_sea, row_index, axis=0)
    surface_kinds = jnp.roll(picked, -lon_shift, axis=1)
    windowed = window_layer(region, surface_kinds, window_gain, window_qkv, window_out)
    retained = lax.dynamic_slice_in_dim(windowed, WIN - lat_shift, rows_dev, 1)
    finished = feed_forward(retained, second_gain, second_in, second_out)
    return jnp.roll(finished, lon_shift, axis=2)


def solution(mesh):
    return jax.shard_map(
        on_device,
        mesh=mesh,
        in_specs=(
            P("member", "space", None, None),
            P(),
            P(),
            P(),
            P(),
            P(),
            P(),
            P(),
            P(),
            P(),
            P(),
            P(),
            P(),
            P(),
            P(),
        ),
        out_specs=P("member", "space", None, None),
        check_vma=False,
    )
```

profile of v0, /device:TPU:1, one launch (start us, length us, event | category | flops | bytes accessed | tf_op | source)
XLA Modules:
  0.0 192.5 jit_solution(3887211586139666257)
XLA Ops:
  0.0 21.9 %all_to_all.8 = bf16[1,8,128,256]{3,2,0,1:T(8,128)(2,1)S(1)} all-to-all(bf16[1,8,128,256]{3,2,0,1:T(8,128)(2,1)} %bitcast.141), channel_id=1, replica_groups=mesh['member'=8,'space'=32] {'member'}, dimensions={1} | all-to-all | bytes 1048576 | tf_op jit(solution)/shard_map/all_to_all | solution.py:110
  21.9 0.2 fusion.55
  22.1 0.4 fusion.58
  22.5 1.0 fusion.60
  23.5 1.7 convolution_convert_fusion.1
  25.2 5.5 %reshape.209 = bf16[128,8,3,8,32]{4,3,2,1,0:T(8,128)(2,1)} reshape(bf16[1024,768]{1,0:T(8,128)(2,1)S(1)} %convolution_convert_fusion.1) | data formatting | bytes 3145728 | tf_op jit(solution)/shard_map/reshape | solution.py:39
  30.7 4.4 %fusion.88 = (bf16[128,8,1,8,32]{4,3,2,1,0:T(8,128)(2,1)S(1)}, bf16[128,8,1,8,32]{4,3,2,1,0:T(8,128)(2,1)S(1)}, bf16[128,8,1,8,32]{4,3,2,1,0:T(8,128)(2,1)S(1)}) fusion(bf16[128,8,3,8,32]{4,3,2,1,0:T(8,128)(2,1)} %reshape.209), kind=kLoop, calls=%fused_computation.142 | loop fusion | bytes 3145728 | tf_op jit(solution)/shard_map/slice | solution.py:50
  35.1 1.2 fusion.27
  36.3 29.3 %fusion.91 = (f32[128,8,8]{2,1,0:T(8,128)S(1)}, f32[128,8,8,8]{2,3,1,0:T(8,128)S(1)}) fusion(f32[128,8,8,8]{2,3,1,0:T(8,128)S(1)} %fusion.27), kind=kOutput, calls=%fused_computation.145 | output fusion | flops 262151 | bytes 557056 | tf_op jit(solution)/shard_map/sub | solution.py:48
  65.6 1.7 convert_bitcast_fusion.1
  67.3 2.7 %copy.159 = bf16[128,8,8,32]{0,3,2,1:T(8,128)(2,1)} copy(bf16[128,8,8,32]{3,1,2,0:T(8,128)(2,1)S(1)} %convert_bitcast_fusion.1) | data formatting | bytes 1048576 | tf_op jit(solution)/shard_map/convert_element_type | solution.py:51
  70.1 1.5 convert_reduce_fusion.1
  71.6 0.4 fusion.45
  72.0 0.3 fusion.47
  72.4 2.8 %fusion.36 = f32[128,8,256]{2,1,0:T(8,128)S(1)} fusion(bf16[1024,256]{1,0:T(8,128)(2,1)S(1)} %copy-done, bf16[256,1024]{1,0:T(8,128)(2,1)} %param.24, bf16[128,8,256]{2,0,1:T(8,128)(2,1)S(1)} %fusion.47), kind=kOutput, calls=%fused_computation.62 | convolution fusion | flops 1083179008 | bytes 2621440 | tf_op jit(solution)/shard_map/dot_general | solution.py:62
  75.1 1.1 fusion.63
  76.3 4.4 %all-to-all-start.1 = ((bf16[8,1,128,256]{3,2,1,0:T(8,128)(2,1)}), bf16[8,1,128,256]{3,2,1,0:T(8,128)(2,1)S(1)}, u32[]{:S(2)}, u32[]{:S(2)}) async-start(bf16[8,1,128,256]{3,2,1,0:T(8,128)(2,1)} %fusion.63), calls=%async_computation.1 | async-start | bytes 1048576 | tf_op jit(solution)/shard_map/all_to_all | solution.py:116
  80.7 0.6 fusion.90
  87.0 0.1 copy.171
  87.2 0.6 gather_fusion
  87.8 7.4 %all-to-all-done.1 = bf16[8,1,128,256]{3,2,1,0:T(8,128)(2,1)S(1)} async-done(((bf16[8,1,128,256]{3,2,1,0:T(8,128)(2,1)}), bf16[8,1,128,256]{3,2,1,0:T(8,128)(2,1)S(1)}, u32[]{:S(2)}, u32[]{:S(2)}) %all-to-all-start.1) | async-done | bytes 524320 | tf_op jit(solution)/shard_map/all_to_all | solution.py:116
  95.2 0.4 fusion.62
  95.6 9.3 %collective-permute-start.1 = (bf16[1,16,64,256]{3,2,1,0:T(8,128)(2,1)S(1)}, bf16[1,16,64,256]{3,2,1,0:T(8,128)(2,1)S(1)}, u32[]{:S(2)}, u32[]{:S(2)}) collective-permute-start(bf16[1,16,64,256]{3,2,1,0:T(8,128)(2,1)S(1)} %fusion.62), channel_id=1, source_target_pairs={{1,0},{2,1},{3,2},{4,3},{5,4},{6,5},{7,6},{8,7},{9,8},{10,9},{11,1... | collective-permute-start | bytes 1572872 | tf_op jit(solution)/shard_map/ppermute | solution.py:23
  105.1 0.1 reshape.213
  106.0 0.5 broadcast_compare_fusion
  106.4 19.0 %collective-permute-done.1 = bf16[1,16,64,256]{3,2,1,0:T(8,128)(2,1)S(1)} collective-permute-done((bf16[1,16,64,256]{3,2,1,0:T(8,128)(2,1)S(1)}, bf16[1,16,64,256]{3,2,1,0:T(8,128)(2,1)S(1)}, u32[]{:S(2)}, u32[]{:S(2)}) %collective-permute-start.1) | collective-permute-done | bytes 524320 | tf_op jit(solution)/shard_map/ppermute | solution.py:23
  125.5 9.9 %collective-permute-done = bf16[1,16,64,256]{3,2,1,0:T(8,128)(2,1)S(1)} collective-permute-done((bf16[1,16,64,256]{3,2,1,0:T(8,128)(2,1)S(1)}, bf16[1,16,64,256]{3,2,1,0:T(8,128)(2,1)S(1)}, u32[]{:S(2)}, u32[]{:S(2)}) %collective-permute-start) | collective-permute-done | bytes 524320 | tf_op jit(solution)/shard_map/ppermute | solution.py:22
  135.4 0.5 fusion.51
  135.9 0.4 fusion.52
  136.4 1.6 convert_bitcast_fusion
  138.1 0.7 multiply_reduce_fusion.1
  138.9 1.8 copy.164
  140.7 0.9 fusion.30
  141.6 2.7 %convolution_convert_fusion = bf16[2048,768]{1,0:T(8,128)(2,1)} fusion(bf16[2048,256]{1,0:T(8,128)(2,1)S(1)} %fusion.30, bf16[256,768]{1,0:T(8,128)(2,1)S(1)} %copy-done.2), kind=kOutput, calls=%fused_computation.33 | convolution fusion | flops 806879232 | bytes 4587520 | tf_op jit(solution)/shard_map/dot_general | solution.py:38
  144.3 4.7 %copy.169 = bf16[2048,768]{0,1:T(8,128)(2,1)} copy(bf16[2048,768]{1,0:T(8,128)(2,1)} %convolution_convert_fusion) | data formatting | bytes 6291456 | tf_op jit(solution)/shard_map/convert_element_type | solution.py:39
  149.0 3.0 %copy.188 = bf16[96,8,8,256]{3,2,1,0:T(8,128)(2,1)S(1)} copy(bf16[96,8,8,256]{3,1,2,0:T(8,128)(2,1)} %bitcast.131) | data formatting | bytes 6291456
  152.0 1.2 fusion.89
  153.2 8.1 %fusion.53 = f32[8,8,256,256]{2,3,1,0:T(8,128)} fusion(bf16[8,256,1,8,32]{1,0,4,3,2:T(8,128)(2,1)S(1)} %get-tuple-element.11, bf16[8,256,1,8,32]{1,0,4,3,2:T(8,128)(2,1)S(1)} %get-tuple-element.10), kind=kOutput, calls=%fused_computation.85 | convolution fusion | flops 268435456 | bytes 18874368 | tf_op jit(solution)/shard_map/bqhd,bkhd->bhqk/dot_general | solution.py:40
  161.2 18.0 %fusion.92 = (f32[8,8,256]{2,1,0:T(8,128)S(1)}, f32[8,8,256,256]{2,3,1,0:T(8,128)}) fusion(f32[8,8,256,256]{2,3,1,0:T(8,128)} %fusion.53, pred[8,256,256]{1,2,0:T(8,128)(4,1)S(1)} %broadcast_compare_fusion), kind=kOutput, calls=%fused_computation.146 | output fusion | flops 25166080 | bytes 34144256 | tf_op jit(solution)/shard_map/sub | solution.py:48
  179.2 7.4 %fusion.33 = bf16[8,8,32,256]{3,2,1,0:T(8,128)(2,1)S(1)} fusion(f32[8,8,256,256]{2,3,1,0:T(8,128)} %get-tuple-element.19, f32[8,8,256]{2,1,0:T(8,128)S(1)} %get-tuple-element.18, bf16[8,256,1,8,32]{1,0,4,3,2:T(8,128)(2,1)} %get-tuple-element.9), kind=kOutput, calls=%fused_computation.59 | convolution fusion | flops 277348352 | bytes 18939904 | tf_op jit(solution)/shard_map/bhqk,bkhd->bqhd/dot_general | solution.py:49
  186.7 0.5 add_convert_fusion
  187.2 0.1 copy.177
  187.3 0.2 convert_reduce_fusion
  187.6 0.4 fusion.42
  188.0 0.3 fusion.44
  188.3 2.8 %fusion.34 = f32[1024,256]{1,0:T(8,128)S(1)} fusion(bf16[1024,256]{1,0:T(8,128)(2,1)} %param.31, bf16[1024,256]{1,0:T(8,128)(2,1)S(1)} %bitcast.142, bf16[256,1024]{1,0:T(8,128)(2,1)} %param.30), kind=kOutput, calls=%fused_computation.60 | convolution fusion | flops 1083179008 | bytes 2621440 | tf_op jit(solution)/shard_map/dot_general | solution.py:62
  191.2 0.1 fusion.49
  191.3 1.2 fusion.61
  (39 shorter events, 0.6 us)
Async XLA Ops:
  0.0 72.3 %copy-start = (bf16[1024,256]{1,0:T(8,128)(2,1)S(1)}, bf16[1024,256]{1,0:T(8,128)(2,1)}, u32[]{:S(2)}) copy-start(bf16[1024,256]{1,0:T(8,128)(2,1)} %param.25) | copy-start | bytes 1572868
  65.6 4.4 %copy-start.5 = (bf16[256,256]{1,0:T(8,128)(2,1)S(1)}, bf16[256,256]{1,0:T(8,128)(2,1)}, u32[]{:S(2)}) copy-start(bf16[256,256]{1,0:T(8,128)(2,1)} %param.22) | copy-start | bytes 393220
  67.3 4.7 %copy-start.7 = (f32[256]{0:T(256)S(1)}, f32[256]{0:T(256)}, u32[]{:S(2)}) copy-start(f32[256]{0:T(256)} %param.23) | copy-start | bytes 3076
  72.3 8.4 %copy-start.6 = (s32[2]{0:T(128)S(1)}, s32[2]{0:T(128)}, u32[]{:S(2)}) copy-start(s32[2]{0:T(128)} %param.18) | copy-start | bytes 28
  72.3 14.7 %copy-start.3 = (s32[512,64]{0,1:T(8,128)S(1)}, s32[512,64]{0,1:T(8,128)}, u32[]{:S(2)}) copy-start(s32[512,64]{0,1:T(8,128)} %param.19) | copy-start | bytes 393220
  76.3 18.9 %all-to-all-start.1 = ((bf16[8,1,128,256]{3,2,1,0:T(8,128)(2,1)}), bf16[8,1,128,256]{3,2,1,0:T(8,128)(2,1)S(1)}, u32[]{:S(2)}, u32[]{:S(2)}) async-start(bf16[8,1,128,256]{3,2,1,0:T(8,128)(2,1)} %fusion.63), calls=%async_computation.1 | async-start | bytes 1048576 | tf_op jit(solution)/shard_map/all_to_all | solution.py:116
  95.6 29.9 %collective-permute-start.1 = (bf16[1,16,64,256]{3,2,1,0:T(8,128)(2,1)S(1)}, bf16[1,16,64,256]{3,2,1,0:T(8,128)(2,1)S(1)}, u32[]{:S(2)}, u32[]{:S(2)}) collective-permute-start(bf16[1,16,64,256]{3,2,1,0:T(8,128)(2,1)S(1)} %fusion.62), channel_id=1, source_target_pairs={{1,0},{2,1},{3,2},{4,3},{5,4},{6,5},{7,6},{8,7},{9,8},{10,9},{11,1... | collective-permute-start | bytes 1572872 | tf_op jit(solution)/shard_map/ppermute | solution.py:23
  104.9 30.5 %collective-permute-start = (bf16[1,16,64,256]{3,2,1,0:T(8,128)(2,1)S(1)}, bf16[1,16,64,256]{3,2,1,0:T(8,128)(2,1)S(1)}, u32[]{:S(2)}, u32[]{:S(2)}) collective-permute-start(bf16[1,16,64,256]{3,2,1,0:T(8,128)(2,1)S(1)} %fusion.62), channel_id=1, source_target_pairs={{0,1},{1,2},{2,3},{3,4},{4,5},{5,6},{6,7},{7,8},{8,9},{9,10},{10,1... | collective-permute-start | bytes 1572872 | tf_op jit(solution)/shard_map/ppermute | solution.py:22
  136.4 4.3 %copy-start.8 = (f32[256]{0:T(256)S(1)}, f32[256]{0:T(256)}, u32[]{:S(2)}) copy-start(f32[256]{0:T(256)} %param.26) | copy-start | bytes 3076
  138.1 3.5 %copy-start.2 = (bf16[256,768]{1,0:T(8,128)(2,1)S(1)}, bf16[256,768]{1,0:T(8,128)(2,1)}, u32[]{:S(2)}) copy-start(bf16[256,768]{1,0:T(8,128)(2,1)} %param.27) | copy-start | bytes 1179652
  179.2 7.5 %copy-start.4 = (bf16[256,256]{1,0:T(8,128)(2,1)S(1)}, bf16[256,256]{1,0:T(8,128)(2,1)}, u32[]{:S(2)}) copy-start(bf16[256,256]{1,0:T(8,128)(2,1)} %param.28) | copy-start | bytes 393220
  186.7 1.3 copy-start.9
  188.3 4.2 %copy-start.1 = (bf16[1024,256]{1,0:T(8,128)(2,1)S(1)}, bf16[1024,256]{1,0:T(8,128)(2,1)}, u32[]{:S(2)}) copy-start(bf16[1024,256]{1,0:T(8,128)(2,1)} %param.25) | copy-start | bytes 1572868
where the time goes:
time: 193 us
  other arithmetic  58.2 us (30%)
  waiting for transfers between devices  36.4 us (19%)
  matrix products  30.4 us (16%)
  local copies, waits for them, and re-layouts  25.1 us (13%)
  blocking collectives  21.9 us (11%)
  starting transfers between devices  13.7 us (7%)
  between operations  6.83 us (4%)
    sub x2, other arithmetic, attend(): weights = jax.nn.softmax(scores, axis=-1).astype(jnp.bfloat16)  47.3 us
    all_to_all x1, blocking collectives, on_device(): lax.all_to_all(grouped, 'member', split_axis=1, concat_axis=0, tiled=True)  21.9 us
    ppermute x1, waiting for transfers between devices, padded(): after = lax.ppermute(leading, axis, down)  19 us
    ppermute x1, waiting for transfers between devices, padded(): before = lax.ppermute(last, axis, up)  9.91 us
    dot_general x2, matrix products, attend(): jnp.einsum('bqhd,bkhd->bhqk', projected[:, :, 0], projected[:, :, 1], pre...  9.31 us
    ppermute x1, starting transfers between devices, padded(): after = lax.ppermute(leading, axis, down)  9.3 us
    dot_general x2, matrix products, attend(): jnp.einsum('bhqk,bkhd->bqhd', weights, projected[:, :, 2], preferred_elem...  9.1 us
    all_to_all x1, waiting for transfers between devices, on_device(): lax.all_to_all(mixed_points, 'member', split_axis=0, concat_axis=1, tiled...  7.42 us
  transfers between devices with their start and end apart: 3, of which 3 were waited for; matrix products, arithmetic and copies ran while one was open for 1% of the time, Pallas kernels for 0%

commit v1 on v0

v1 whole, which is shorter than its diff:
```python
import math

import jax
import jax.numpy as jnp
from jax import lax
from jax.experimental import pallas as pl
from jax.experimental.pallas import tpu as pltpu
from jax.sharding import PartitionSpec as P

HEADS = 8
WIN = 16
EPSILON = 1e-05
BLOCK = 256
FAR = 1e30


def normalise(values, gains):
    center = jnp.mean(values, axis=-1, keepdims=True)
    shifted = values - center
    spread = jnp.mean(shifted * shifted, axis=-1, keepdims=True)
    return (shifted * lax.rsqrt(spread + EPSILON) * gains).astype(jnp.bfloat16)


def wide_dot(a, b):
    return jnp.dot(a, b, preferred_element_type=jnp.float32)


def gelu(x):
    inner = x * (0.7978845608028654 + 0.035677408136300125 * (x * x))
    return (x * (0.5 + 0.5 * jnp.tanh(inner))).astype(jnp.bfloat16)


def feed_forward(stream, gain_ref, in_ref, out_ref):
    wide = stream.astype(jnp.float32)
    normed = normalise(wide, gain_ref[...])
    hidden_size = in_ref.shape[1]
    total = wide
    for start in range(0, hidden_size, BLOCK):
        hidden = gelu(wide_dot(normed, in_ref[:, start : start + BLOCK]))
        total = total + wide_dot(hidden, out_ref[start : start + BLOCK, :])
    return total.astype(jnp.bfloat16)


def member_kernel(x_ref, gain_ref, qkv_ref, out_ref, gain2_ref, in2_ref, out2_ref, o_ref):
    members, points, features = x_ref.shape
    tokens = members * points
    size = features // HEADS
    stream = x_ref[...].astype(jnp.float32).reshape(tokens, features)
    normed = normalise(stream, gain_ref[...])
    query = wide_dot(normed, qkv_ref[:, :features]).astype(jnp.bfloat16)
    key = wide_dot(normed, qkv_ref[:, features : 2 * features]).astype(jnp.bfloat16)
    value = wide_dot(normed, qkv_ref[:, 2 * features :])
    query = query.reshape(members, points, features)
    key = key.reshape(members, points, features)
    value = value.astype(jnp.bfloat16).astype(jnp.float32).reshape(members, points, features)

    lane = lax.broadcasted_iota(jnp.int32, (features, 128), 1) % 64
    head = lax.broadcasted_iota(jnp.int32, (features, 128), 0) // size
    place = lane - head
    scores = jnp.zeros((tokens, 128), jnp.float32)
    for j in range(members):
        pick = jnp.where((place == j * HEADS) & (lane // HEADS == j), 1.0, 0.0).astype(jnp.bfloat16)
        product = (query * key[j][None]).reshape(tokens, features)
        scores = scores + wide_dot(product, pick)
    top = scores
    for step in (8, 16, 32):
        top = jnp.maximum(top, pltpu.roll(top, step, 1))
    weights = jnp.exp((scores - top) * (1.0 / math.sqrt(size)))
    total = weights
    for step in (8, 16, 32):
        total = total + pltpu.roll(total, step, 1)
    weights = (weights / total).astype(jnp.bfloat16)

    lane = lax.broadcasted_iota(jnp.int32, (128, features), 0)
    head = lax.broadcasted_iota(jnp.int32, (128, features), 1) // size
    place = lane - head
    mixed = jnp.zeros((members, points, features), jnp.float32)
    for j in range(members):
        spread = jnp.where(place == j * HEADS, 1.0, 0.0).astype(jnp.bfloat16)
        widened = wide_dot(weights, spread).reshape(members, points, features)
        mixed = mixed + widened * value[j][None]
    mixed = mixed.reshape(tokens, features).astype(jnp.bfloat16)
    stream = (stream + wide_dot(mixed, out_ref[...])).astype(jnp.bfloat16)
    result = feed_forward(stream, gain2_ref, in2_ref, out2_ref)
    o_ref[...] = result.reshape(members, points, features)


def window_kernel(
    place_ref, x_ref, kinds_ref, gain_ref, qkv_ref, out_ref, gain2_ref, in2_ref, out2_ref, o_ref
):
    rows, longitudes, features = x_ref.shape
    windows = longitudes // WIN
    size = features // HEADS
    half = features // 2
    tokens = WIN * WIN
    lat_shift = place_ref[0]
    lon_shift = place_ref[1]
    w = pl.program_id(0)
    here = pl.ds(pl.multiple_of(w * WIN, WIN), WIN)
    following = lax.rem(w + 1, windows)
    there = pl.ds(pl.multiple_of(following * WIN, WIN), WIN)

    column = lax.broadcasted_iota(jnp.int32, (WIN, WIN, features), 1)
    inside = column >= lon_shift
    stream = jnp.where(
        inside, x_ref[:, here, :].astype(jnp.float32), x_ref[:, there, :].astype(jnp.float32)
    ).reshape(tokens, features)

    upper = kinds_ref[place_ref[2]].astype(jnp.float32)
    lower = kinds_ref[place_ref[3]].astype(jnp.float32)
    row = lax.broadcasted_iota(jnp.int32, (rows, longitudes), 0)
    kinds = jnp.where(row >= lat_shift, upper, lower)
    kinds = jnp.broadcast_to(kinds[:, None, :], (WIN, WIN, longitudes))
    column = lax.broadcasted_iota(jnp.int32, (WIN, WIN, longitudes), 1)
    lane = lax.broadcasted_iota(jnp.int32, (WIN, WIN, longitudes), 2)
    wanted = jnp.where(column >= lon_shift, w * WIN, following * WIN) + column
    kinds = jnp.where(lane == wanted, kinds, 0.0).reshape(tokens, longitudes)
    kind = jnp.sum(kinds, axis=-1, keepdims=True)
    kind = jnp.broadcast_to(kind, (tokens, features))

    normed = normalise(stream, gain_ref[...])
    query = wide_dot(normed, qkv_ref[:, :features])
    key = wide_dot(normed, qkv_ref[:, features : 2 * features])
    value = wide_dot(normed, qkv_ref[:, 2 * features :])

    lane = lax.broadcasted_iota(jnp.int32, (tokens, features), 1)
    query_marks, key_marks = [], []
    for first in (features - size, 0):
        query_marks.append(
            jnp.where(
                lane == first, -FAR * kind, jnp.where(lane == first + 1, -FAR * (1.0 - kind), 0.0)
            )
        )
        marked = jnp.where(lane == first, 1.0 - kind, jnp.where(lane == first + 1, kind, 0.0))
        free = (lane >= first) & (lane < first + size)
        key_marks.append(jnp.where(free, marked, key).astype(jnp.bfloat16))
    scale = 1.0 / math.sqrt(size)
    outputs = []
    for group in range(2):
        total = jnp.zeros((tokens, features), jnp.float32)
        for h in range(group * HEADS // 2, (group + 1) * HEADS // 2):
            own = (lane >= h * size) & (lane < (h + 1) * size)
            q = jnp.where(own, query, query_marks[group]).astype(jnp.bfloat16)
            scores = lax.dot_general(
                q, key_marks[group], (((1,), (1,)), ((), ())), preferred_element_type=jnp.float32
            )
            top = jnp.max(scores, axis=-1, keepdims=True)
            weights = jnp.exp((scores - top) * scale).astype(jnp.bfloat16)
            opposite = h * size + (half if group == 0 else -half)
            ones = (lane >= opposite) & (lane < opposite + size)
            v = jnp.where(own, value, jnp.where(ones, 1.0, 0.0)).astype(jnp.bfloat16)
            total = total + wide_dot(weights, v)
        if group == 0:
            outputs.append(total[:, :half] / total[:, half:])
        else:
            outputs.append(total[:, half:] / total[:, :half])
    mixed = jnp.concatenate(outputs, axis=-1).astype(jnp.bfloat16)
    stream = (stream + wide_dot(mixed, out_ref[...])).astype(jnp.bfloat16)
    result = feed_forward(stream, gain2_ref, in2_ref, out2_ref).astype(jnp.float32)
    result = result.reshape(WIN, WIN, features)
    column = lax.broadcasted_iota(jnp.int32, (WIN, WIN, features), 1)
    inside = column >= lon_shift
    kept = o_ref[:, here, :].astype(jnp.float32)
    o_ref[:, here, :] = jnp.where(inside, result, kept).astype(jnp.bfloat16)
    kept = o_ref[:, there, :].astype(jnp.float32)
    o_ref[:, there, :] = jnp.where(inside, kept, result).astype(jnp.bfloat16)


def whole(array):
    return pl.BlockSpec(array.shape, lambda b, n=array.ndim: (0,) * n)


def member_layer(points, *params):
    members, count, features = points.shape
    block = BLOCK // members
    spec = pl.BlockSpec((members, block, features), lambda b: (0, b, 0))
    return pl.pallas_call(
        member_kernel,
        grid=(count // block,),
        out_shape=jax.ShapeDtypeStruct(points.shape, jnp.bfloat16),
        in_specs=[spec] + [whole(p) for p in params],
        out_specs=spec,
        compiler_params=pltpu.CompilerParams(vmem_limit_bytes=32 * 2**20),
    )(points, *params)


def window_layer(place, region, kinds, *params):
    return pl.pallas_call(
        window_kernel,
        grid=(region.shape[1] // WIN,),
        out_shape=jax.ShapeDtypeStruct(region.shape, jnp.bfloat16),
        in_specs=[pl.BlockSpec(memory_space=pltpu.SMEM)]
        + [whole(a) for a in (region, kinds) + params],
        out_specs=whole(region),
        compiler_params=pltpu.CompilerParams(vmem_limit_bytes=32 * 2**20),
    )(place, region, kinds, *params)


def on_device(
    ensemble,
    shifts,
    land_sea,
    member_gain,
    member_qkv,
    member_out,
    first_gain,
    first_in,
    first_out,
    window_gain,
    window_qkv,
    window_out,
    second_gain,
    second_in,
    second_out,
):
    _, rows, longitudes, features = ensemble.shape
    half = rows // 2
    members = lax.axis_size("member")
    spaces = lax.axis_size("space")
    space = lax.axis_index("space")
    up = [(i, (i + 1) % spaces) for i in range(spaces)]
    down = [(j, i) for i, j in up]
    lat_shift, lon_shift = shifts[0], shifts[1]
    kinds = land_sea.reshape(spaces, rows, longitudes)
    own = ensemble[0]
    row = jnp.arange(rows, dtype=jnp.int32)[:, None, None]
    gains = [g.reshape(1, features) for g in (member_gain, first_gain, window_gain, second_gain)]

    def run(window_below):
        if window_below:
            other = lax.ppermute(own[:half], "space", down)
            low = jnp.where(row[:half] >= lat_shift, own[:half], other)
            merged = jnp.concatenate([low, own[half:]])
            blocks = (space, lax.rem(space + 1, spaces))
        else:
            other = lax.ppermute(own[half:], "space", up)
            high = jnp.where(row[half:] >= lat_shift, other, own[half:])
            merged = jnp.concatenate([own[:half], high])
            blocks = (lax.rem(space + spaces - 1, spaces), space)
        parts = merged.reshape(members, -1, features)
        points = lax.all_to_all(parts, "member", split_axis=0, concat_axis=0, tiled=True)
        points = member_layer(
            points, gains[0], member_qkv, member_out, gains[1], first_in, first_out
        )
        region = lax.all_to_all(points, "member", split_axis=0, concat_axis=0, tiled=True)
        place = jnp.stack([lat_shift, lon_shift, blocks[0], blocks[1]]).astype(jnp.int32)
        result = window_layer(
            place,
            region.reshape(rows, longitudes, features),
            kinds,
            gains[2],
            window_qkv,
            window_out,
            gains[3],
            second_in,
            second_out,
        )
        if window_below:
            back = lax.ppermute(result[:half], "space", up)
            low = jnp.where(row[:half] >= lat_shift, result[:half], back)
            return jnp.concatenate([low, result[half:]])
        back = lax.ppermute(result[half:], "space", down)
        high = jnp.where(row[half:] >= lat_shift, back, result[half:])
        return jnp.concatenate([result[:half], high])

    out = lax.cond(lat_shift <= half, lambda: run(True), lambda: run(False))
    return out[None]


def solution(mesh):
    return jax.shard_map(
        on_device,
        mesh=mesh,
        in_specs=(P("member", "space", None, None),) + (P(),) * 14,
        out_specs=P("member", "space", None, None),
        check_vma=False,
    )
```

time: 193 us -> 105 us (0.54)
  other arithmetic: 58.2 us -> 2.2 us
  matrix products: 30.4 us -> 0 us
  local copies, waits for them, and re-layouts: 25.1 us -> 4.97 us
  Pallas kernels: 0 us -> 19.6 us
  between operations: 6.83 us -> 0.67 us
  waiting for transfers between devices: 36.4 us -> 42 us
  starting transfers between devices: 13.7 us -> 17.1 us
  blocking collectives: 21.9 us -> 18.5 us
    sub x2 -> x0, other arithmetic: 47.3 us -> none  [attend(): weights = jax.nn.softmax(scores, axis=-1).astype(jnp.bfloat16)]
    dot_general x10 -> x0, matrix products: 30.4 us -> none  [the longest x2 9.31 us: attend(): jnp.einsum('bqhd,bkhd->bhqk', projected[:, :, 0], projected[:, :, 1], pre...]
    pallas_call x0 -> x2, Pallas kernels: none -> 19.6 us  [the longest x1 10.3 us: member_layer(): pl.pallas_call(member_kernel, grid=(count // block,), out_shape=jax.Shape...]
    convert_element_type x3 -> x0, local copies, waits for them, and re-layouts: 9.27 us -> none  [the longest x1 4.71 us: attend(): projected.astype(jnp.bfloat16).reshape(groups, length, 3, HEADS, head_size)]
    all_to_all x1, waiting for transfers between devices: 7.42 us -> 13.2 us  [run(): lax.all_to_all(points, 'member', split_axis=0, concat_axis=0, tiled=True)]
    reshape x2 -> x0, local copies, waits for them, and re-layouts: 5.61 us -> none  [the longest x1 5.51 us: attend(): projected.astype(jnp.bfloat16).reshape(groups, length, 3, HEADS, head_size)]
    convert_element_type x6 -> x0, other arithmetic: 4.37 us -> none  [the longest x4 2.58 us: layer_norm(): ((values - center) * lax.rsqrt(spread + EPSILON) * gains).astype(jnp.bflo...]
    slice x3, local copies, waits for them, and re-layouts: 6.14 us -> 2.44 us  [the longest x1 1.38 us: on_device(): lat_shift, lon_shift = (shifts[0], shifts[1])]
  transfers between devices with their start and end apart: 3 -> 3, of which waited for: 3 -> 3; matrix products, arithmetic and copies ran while one was open for 1% -> 2% of each run, Pallas kernels for 0% -> 0%
where the time goes in v1:
time: 105 us
  waiting for transfers between devices  42 us (40%)
  Pallas kernels  19.6 us (19%)
  blocking collectives  18.5 us (18%)
  starting transfers between devices  17.1 us (16%)
  local copies, waits for them, and re-layouts  4.97 us (5%)
  other arithmetic  2.2 us (2%)
    ppermute x1, waiting for transfers between devices, run(): back = lax.ppermute(result[:half], 'space', up)  19 us
    all_to_all x1, blocking collectives, run(): lax.all_to_all(parts, 'member', split_axis=0, concat_axis=0, tiled=True)  18.5 us
    all_to_all x1, waiting for transfers between devices, run(): lax.all_to_all(points, 'member', split_axis=0, concat_axis=0, tiled=True)  13.2 us
    ppermute x1, starting transfers between devices, run(): other = lax.ppermute(own[:half], 'space', down)  12.5 us
    pallas_call x1, Pallas kernels, member_layer(): pl.pallas_call(member_kernel, grid=(count // block,), out_shape=jax.Shape...  10.3 us
    ppermute x1, waiting for transfers between devices, run(): other = lax.ppermute(own[:half], 'space', down)  9.8 us
    pallas_call x1, Pallas kernels, window_layer(): pl.pallas_call(window_kernel, grid=(region.shape[1] // WIN,), out_shape=j...  9.34 us
    all_to_all x1, starting transfers between devices, run(): lax.all_to_all(points, 'member', split_axis=0, concat_axis=0, tiled=True)  4.57 us
  transfers between devices with their start and end apart: 3, of which 3 were waited for; matrix products, arithmetic and copies ran while one was open for 2% of the time, Pallas kernels for 0%

profile of v1, /device:TPU:1, one launch (start us, length us, event | category | flops | bytes accessed | tf_op | source)
XLA Modules:
  0.0 105.2 jit_solution(16368683707724857652)
XLA Ops:
  0.0 0.0 copy-start.10
  0.0 1.4 %fusion.2 = (s32[1]{0:T(128)}, s32[1]{0:T(128)}) fusion(s32[2]{0:T(128)} %param.18), kind=kLoop, calls=%fused_computation.14 | loop fusion | bytes 16 | tf_op jit(solution)/shard_map/slice | solution.py:223
  2.0 0.0 copy-start.19
  2.0 0.0 copy-start.20
  2.0 0.0 copy-start.21
  2.0 1.0 copy.18
  3.0 0.0 copy-start.18
  3.1 0.0 copy-done.10
  3.1 0.0 copy-done.19
  3.1 0.0 copy-done.20
  3.1 0.0 copy-done.21
  3.1 0.6 copy-done.18
  3.7 100.6 %conditional.1 = (bf16[1,16,64,256]{3,2,1,0:T(8,128)(2,1)S(1)}) conditional(s32[]{:T(128)} %convert_element_type.3, (s32[]{:T(128)}, s32[1]{0:T(128)}, s32[1]{0:T(128)}, bf16[16,64,256]{2,1,0:T(8,128)(2,1)}, s32[16,1,1]{0,2,1:T(1,128)S(1)}, /*index=5*/s32[]{:T(128)}, f32[1,256]{1,0:T(1,128)S(1)}, bf16[256,768]{1,0:T(8,128)(2,1)S(1)}, ...), branch_computations={%region_0.1_spmd, %region_1.2_spmd} | conditional | flops 786459 | bytes 23593472 | solution.py:266
  3.7 0.0 copy-start.1
  3.7 1.0 slice.36
  4.8 12.5 %collective-permute-start = (bf16[8,64,256]{2,1,0:T(8,128)(2,1)S(1)}, bf16[8,64,256]{2,1,0:T(8,128)(2,1)S(1)}, u32[]{:S(2)}, u32[]{:S(2)}) collective-permute-start(bf16[8,64,256]{2,1,0:T(8,128)(2,1)S(1)} %slice.36), channel_id=1, source_target_pairs={{1,0},{2,1},{3,2},{4,3},{5,4},{6,5},{7,6},{8,7},{9,8},{10,9},{11,1... | collective-permute-start | bytes 786440 | tf_op jit(solution)/shard_map/cond/branch_1_fun/ppermute | solution.py:231
  17.2 0.6 compare_bitcast_fusion.1
  17.8 9.8 %collective-permute-done = bf16[8,64,256]{2,1,0:T(8,128)(2,1)S(1)} collective-permute-done((bf16[8,64,256]{2,1,0:T(8,128)(2,1)S(1)}, bf16[8,64,256]{2,1,0:T(8,128)(2,1)S(1)}, u32[]{:S(2)}, u32[]{:S(2)}) %collective-permute-start) | collective-permute-done | bytes 262176 | tf_op jit(solution)/shard_map/cond/branch_1_fun/ppermute | solution.py:231
  27.6 0.0 copy-done.1
  27.6 0.1 broadcast_select_fusion.3
  27.7 0.0 copy-start.14
  27.8 0.0 copy-start.3
  27.8 0.0 copy-start.5
  27.8 18.5 %all_to_all.17.x_ref = bf16[8,128,256]{2,1,0:T(8,128)(2,1)S(1)} all-to-all(bf16[8,128,256]{2,1,0:T(8,128)(2,1)S(1)} %bitcast.30), channel_id=1, replica_groups=mesh['member'=8,'space'=32] {'member'}, dimensions={0} | all-to-all | bytes 1048576 | tf_op jit(solution)/shard_map/cond/branch_1_fun/all_to_all | solution.py:241
  46.4 0.0 copy-done.14
  46.4 0.0 copy-done.3
  46.4 0.0 copy-done.5
  46.4 0.0 copy-start.12
  46.4 0.0 copy-start.16
  46.4 10.3 %branch_1_fun.2 = bf16[8,128,256]{2,1,0:T(8,128)(2,1)} custom-call(bf16[8,128,256]{2,1,0:T(8,128)(2,1)S(1)} %all_to_all.17.x_ref, f32[1,256]{1,0:T(1,128)S(1)} %get-tuple-element.110.gain_ref, bf16[256,768]{1,0:T(8,128)(2,1)S(1)} %get-tuple-element.111.qkv_ref, bf16[256,256]{1,0:T(8,128)(2,1)S(1)} %copy-done.14, f32[1,256]{1,0:T(1,128)S(1)} %get-tuple-element.113.gain2_ref, ...), custom_call_target="tpu_custom_call" | custom-call | tf_op jit(solution)/shard_map/cond/branch_1_fun/pallas_call | solution.py:177
  56.7 0.0 copy-start.7
  56.7 0.0 copy-start.9
  56.7 4.6 %all-to-all-start.1 = ((bf16[8,128,256]{2,1,0:T(8,128)(2,1)}), bf16[8,128,256]{2,1,0:T(8,128)(2,1)S(1)}, u32[]{:S(2)}, u32[]{:S(2)}) async-start(bf16[8,128,256]{2,1,0:T(8,128)(2,1)} %branch_1_fun.2), calls=%async_computation.1 | async-start | bytes 1048576 | tf_op jit(solution)/shard_map/cond/branch_1_fun/all_to_all | solution.py:245
  61.2 1.3 %pad_add_fusion.1.place_ref = s32[4]{0:T(128)S(1)} fusion(s32[1]{0:T(128)} %bitcast.8, s32[1]{0:T(128)} %bitcast.7, s32[1]{0:T(128)} %get-tuple-element.107, s32[1]{0:T(128)} %get-tuple-element.106), kind=kLoop, calls=%fused_computation.11 | loop fusion | flops 12 | bytes 32 | tf_op jit(solution)/shard_map/cond/branch_1_fun/stack | solution.py:246
  62.5 13.2 %all-to-all-done.1 = bf16[8,128,256]{2,1,0:T(8,128)(2,1)S(1)} async-done(((bf16[8,128,256]{2,1,0:T(8,128)(2,1)}), bf16[8,128,256]{2,1,0:T(8,128)(2,1)S(1)}, u32[]{:S(2)}, u32[]{:S(2)}) %all-to-all-start.1) | async-done | bytes 524320 | tf_op jit(solution)/shard_map/cond/branch_1_fun/all_to_all | solution.py:245
  75.7 0.0 copy-done.12
  75.7 0.0 copy-done.16
  75.7 0.0 copy-done.7
  75.8 0.0 copy-done.9
  75.8 9.3 %branch_1_fun.3 = bf16[16,64,256]{2,1,0:T(8,128)(2,1)S(1)} custom-call(s32[4]{0:T(128)S(1)} %pad_add_fusion.1.place_ref, bf16[16,64,256]{2,1,0:T(8,128)(2,1)S(1)} %bitcast.23, s32[32,16,64]{2,1,0:T(8,128)S(1)} %get-tuple-element.116.kinds_ref, f32[1,256]{1,0:T(1,128)S(1)} %get-tuple-element.117.gain_ref, bf16[256,768]{1,0:T(8,128)(2,1)S(1)} %copy-done.12, ...), custom_call_target="tpu_custom_call" | custom-call | tf_op jit(solution)/shard_map/cond/branch_1_fun/pallas_call | solution.py:188
  85.1 0.1 collective-permute-start.1
  85.2 19.0 %collective-permute-done.1 = bf16[8,64,256]{2,1,0:T(8,128)(2,1)S(1)} collective-permute-done((bf16[8,64,256]{2,1,0:T(8,128)(2,1)S(1)}, bf16[8,64,256]{2,1,0:T(8,128)(2,1)S(1)}, u32[]{:S(2)}, u32[]{:S(2)}) %collective-permute-start.1) | collective-permute-done | bytes 262176 | tf_op jit(solution)/shard_map/cond/branch_1_fun/ppermute | solution.py:259
  104.2 0.1 broadcast_select_fusion.2
  104.4 0.0 copy-start.17
  104.4 0.8 copy-done.17
  (5 shorter events, 0.1 us)
Async XLA Ops:
  0.0 3.1 %copy-start.10 = (bf16[256,768]{1,0:T(8,128)(2,1)S(1)}, bf16[256,768]{1,0:T(8,128)(2,1)}, u32[]{:S(2)}) copy-start(bf16[256,768]{1,0:T(8,128)(2,1)} %param.21) | copy-start | bytes 1179652
  2.0 1.1 %copy-start.19 = (f32[256]{0:T(256)S(1)}, f32[256]{0:T(256)}, u32[]{:S(2)}) copy-start(f32[256]{0:T(256)} %param.23) | copy-start | bytes 3076
  2.0 1.1 %copy-start.20 = (f32[256]{0:T(256)S(1)}, f32[256]{0:T(256)}, u32[]{:S(2)}) copy-start(f32[256]{0:T(256)} %param.26) | copy-start | bytes 3076
  2.0 1.1 %copy-start.21 = (f32[256]{0:T(256)S(1)}, f32[256]{0:T(256)}, u32[]{:S(2)}) copy-start(f32[256]{0:T(256)} %param.29) | copy-start | bytes 3076
  3.0 0.7 copy-start.18
  3.7 23.9 %copy-start.1 = (bf16[16,64,256]{2,1,0:T(8,128)(2,1)S(1)}, bf16[16,64,256]{2,1,0:T(8,128)(2,1)}, u32[]{:S(2)}) copy-start(bf16[16,64,256]{2,1,0:T(8,128)(2,1)} %get-tuple-element.109) | copy-start | bytes 1572868 | tf_op jit(solution)/shard_map/cond
  4.8 22.8 %collective-permute-start = (bf16[8,64,256]{2,1,0:T(8,128)(2,1)S(1)}, bf16[8,64,256]{2,1,0:T(8,128)(2,1)S(1)}, u32[]{:S(2)}, u32[]{:S(2)}) collective-permute-start(bf16[8,64,256]{2,1,0:T(8,128)(2,1)S(1)} %slice.36), channel_id=1, source_target_pairs={{1,0},{2,1},{3,2},{4,3},{5,4},{6,5},{7,6},{8,7},{9,8},{10,9},{11,1... | collective-permute-start | bytes 786440 | tf_op jit(solution)/shard_map/cond/branch_1_fun/ppermute | solution.py:231
  27.7 18.6 %copy-start.14 = (bf16[256,256]{1,0:T(8,128)(2,1)S(1)}, bf16[256,256]{1,0:T(8,128)(2,1)}, u32[]{:S(2)}) copy-start(bf16[256,256]{1,0:T(8,128)(2,1)} %get-tuple-element.112.out_ref) | copy-start | bytes 393220 | tf_op jit(solution)/shard_map/cond
  27.8 18.6 %copy-start.3 = (bf16[256,1024]{1,0:T(8,128)(2,1)S(1)}, bf16[256,1024]{1,0:T(8,128)(2,1)}, u32[]{:S(2)}) copy-start(bf16[256,1024]{1,0:T(8,128)(2,1)} %get-tuple-element.114.in2_ref) | copy-start | bytes 1572868 | tf_op jit(solution)/shard_map/cond
  27.8 18.6 %copy-start.5 = (bf16[1024,256]{1,0:T(8,128)(2,1)S(1)}, bf16[1024,256]{1,0:T(8,128)(2,1)}, u32[]{:S(2)}) copy-start(bf16[1024,256]{1,0:T(8,128)(2,1)} %get-tuple-element.115.out2_ref) | copy-start | bytes 1572868 | tf_op jit(solution)/shard_map/cond
  46.4 29.4 %copy-start.12 = (bf16[256,768]{1,0:T(8,128)(2,1)S(1)}, bf16[256,768]{1,0:T(8,128)(2,1)}, u32[]{:S(2)}) copy-start(bf16[256,768]{1,0:T(8,128)(2,1)} %get-tuple-element.118.qkv_ref) | copy-start | bytes 1179652 | tf_op jit(solution)/shard_map/cond
  46.4 29.4 %copy-start.16 = (bf16[256,256]{1,0:T(8,128)(2,1)S(1)}, bf16[256,256]{1,0:T(8,128)(2,1)}, u32[]{:S(2)}) copy-start(bf16[256,256]{1,0:T(8,128)(2,1)} %get-tuple-element.119.out_ref) | copy-start | bytes 393220 | tf_op jit(solution)/shard_map/cond
  56.7 19.1 %copy-start.7 = (bf16[256,1024]{1,0:T(8,128)(2,1)S(1)}, bf16[256,1024]{1,0:T(8,128)(2,1)}, u32[]{:S(2)}) copy-start(bf16[256,1024]{1,0:T(8,128)(2,1)} %get-tuple-element.121.in2_ref) | copy-start | bytes 1572868 | tf_op jit(solution)/shard_map/cond
  56.7 19.1 %copy-start.9 = (bf16[1024,256]{1,0:T(8,128)(2,1)S(1)}, bf16[1024,256]{1,0:T(8,128)(2,1)}, u32[]{:S(2)}) copy-start(bf16[1024,256]{1,0:T(8,128)(2,1)} %get-tuple-element.122.out2_ref) | copy-start | bytes 1572868 | tf_op jit(solution)/shard_map/cond
  56.7 19.1 %all-to-all-start.1 = ((bf16[8,128,256]{2,1,0:T(8,128)(2,1)}), bf16[8,128,256]{2,1,0:T(8,128)(2,1)S(1)}, u32[]{:S(2)}, u32[]{:S(2)}) async-start(bf16[8,128,256]{2,1,0:T(8,128)(2,1)} %branch_1_fun.2), calls=%async_computation.1 | async-start | bytes 1048576 | tf_op jit(solution)/shard_map/cond/branch_1_fun/all_to_all | solution.py:245
  85.1 19.1 %collective-permute-start.1 = (bf16[8,64,256]{2,1,0:T(8,128)(2,1)S(1)}, bf16[8,64,256]{2,1,0:T(8,128)(2,1)S(1)}, u32[]{:S(2)}, u32[]{:S(2)}) collective-permute-start(bf16[8,64,256]{2,1,0:T(8,128)(2,1)S(1)} %slice.46), channel_id=1, source_target_pairs={{0,1},{1,2},{2,3},{3,4},{4,5},{5,6},{6,7},{7,8},{8,9},{9,10},{10,1... | collective-permute-start | bytes 786440 | tf_op jit(solution)/shard_map/cond/branch_1_fun/ppermute | solution.py:259
  104.4 0.8 copy-start.17

commit v2 on v1

--- a/solution.py
+++ b/solution.py
@@ -86,9 +86,19 @@
 
 
 def window_kernel(
-    place_ref, x_ref, kinds_ref, gain_ref, qkv_ref, out_ref, gain2_ref, in2_ref, out2_ref, o_ref
+    place_ref,
+    low_ref,
+    high_ref,
+    kinds_ref,
+    gain_ref,
+    qkv_ref,
+    out_ref,
+    gain2_ref,
+    in2_ref,
+    out2_ref,
+    o_ref,
 ):
-    rows, longitudes, features = x_ref.shape
+    rows, longitudes, features = o_ref.shape
     windows = longitudes // WIN
     size = features // HEADS
     half = features // 2
@@ -102,9 +112,11 @@
 
     column = lax.broadcasted_iota(jnp.int32, (WIN, WIN, features), 1)
     inside = column >= lon_shift
-    stream = jnp.where(
-        inside, x_ref[:, here, :].astype(jnp.float32), x_ref[:, there, :].astype(jnp.float32)
-    ).reshape(tokens, features)
+    region = [
+        jnp.concatenate([low_ref[:, at, :], high_ref[:, at, :]]).astype(jnp.float32)
+        for at in (here, there)
+    ]
+    stream = jnp.where(inside, *region).reshape(tokens, features)
 
     upper = kinds_ref[place_ref[2]].astype(jnp.float32)
     lower = kinds_ref[place_ref[3]].astype(jnp.float32)
@@ -181,19 +193,27 @@
         in_specs=[spec] + [whole(p) for p in params],
         out_specs=spec,
         compiler_params=pltpu.CompilerParams(vmem_limit_bytes=32 * 2**20),
+        cost_estimate=pl.CostEstimate(
+            flops=16 * 10**8, bytes_accessed=3 * 2**20, transcendentals=6 * 10**5
+        ),
     )(points, *params)
 
 
-def window_layer(place, region, kinds, *params):
+def window_layer(place, low, high, kinds, *params):
+    half, longitudes, features = low.shape
+    region = (2 * half, longitudes, features)
     return pl.pallas_call(
         window_kernel,
-        grid=(region.shape[1] // WIN,),
-        out_shape=jax.ShapeDtypeStruct(region.shape, jnp.bfloat16),
+        grid=(longitudes // WIN,),
+        out_shape=jax.ShapeDtypeStruct(region, jnp.bfloat16),
         in_specs=[pl.BlockSpec(memory_space=pltpu.SMEM)]
-        + [whole(a) for a in (region, kinds) + params],
-        out_specs=whole(region),
+        + [whole(a) for a in (low, high, kinds) + params],
+        out_specs=pl.BlockSpec(region, lambda b: (0, 0, 0)),
         compiler_params=pltpu.CompilerParams(vmem_limit_bytes=32 * 2**20),
-    )(place, region, kinds, *params)
+        cost_estimate=pl.CostEstimate(
+            flops=4 * 10**9, bytes_accessed=3 * 2**20, transcendentals=4 * 10**6
+        ),
+    )(place, low, high, kinds, *params)
 
 
 def on_device(
@@ -229,24 +249,28 @@
     def run(window_below):
         if window_below:
             other = lax.ppermute(own[:half], "space", down)
-            low = jnp.where(row[:half] >= lat_shift, own[:half], other)
-            merged = jnp.concatenate([low, own[half:]])
+            merged_half = jnp.where(row[:half] >= lat_shift, own[:half], other)
+            whole_half = own[half:]
             blocks = (space, lax.rem(space + 1, spaces))
         else:
             other = lax.ppermute(own[half:], "space", up)
-            high = jnp.where(row[half:] >= lat_shift, other, own[half:])
-            merged = jnp.concatenate([own[:half], high])
+            merged_half = jnp.where(row[half:] >= lat_shift, other, own[half:])
+            whole_half = own[:half]
             blocks = (lax.rem(space + spaces - 1, spaces), space)
-        parts = merged.reshape(members, -1, features)
-        points = lax.all_to_all(parts, "member", split_axis=0, concat_axis=0, tiled=True)
-        points = member_layer(
-            points, gains[0], member_qkv, member_out, gains[1], first_in, first_out
-        )
-        region = lax.all_to_all(points, "member", split_axis=0, concat_axis=0, tiled=True)
-        place = jnp.stack([lat_shift, lon_shift, blocks[0], blocks[1]]).astype(jnp.int32)
+        place = jnp.stack([lat_shift, lon_shift, *blocks]).astype(jnp.int32)
+
+        def mixed(chunk):
+            points = lax.all_to_all(chunk, "member", split_axis=0, concat_axis=0, tiled=True)
+            points = member_layer(
+                points, gains[0], member_qkv, member_out, gains[1], first_in, first_out
+            )
+            return lax.all_to_all(points, "member", split_axis=0, concat_axis=0, tiled=True)
+
+        settled = mixed(whole_half)
+        halves = [mixed(merged_half), settled] if window_below else [settled, mixed(merged_half)]
         result = window_layer(
             place,
-            region.reshape(rows, longitudes, features),
+            *halves,
             kinds,
             gains[2],
             window_qkv,

time: 105 us -> 111 us (1.057); the launches traced: 105 us -> 110 us
  starting transfers between devices: 17.1 us -> 25.6 us
  blocking collectives: 18.5 us -> 12.9 us
    all_to_all x1 -> x3, starting transfers between devices: 4.57 us -> 13.1 us  [the longest x2 8.71 us: mixed(): lax.all_to_all(points, 'member', split_axis=0, concat_axis=0, tiled=True)]
    all_to_all x1, blocking collectives: 18.5 us -> 12.9 us  [mixed(): lax.all_to_all(chunk, 'member', split_axis=0, concat_axis=0, tiled=True)]
    pallas_call x1 -> x2, Pallas kernels: 10.3 us -> 10.9 us  [member_layer(): pl.pallas_call(member_kernel, grid=(count // block,), out_shape=jax.Shape...]
    all_to_all x1 -> x3, waiting for transfers between devices: 13.2 us -> 13.8 us  [the longest x2 10.6 us: mixed(): lax.all_to_all(points, 'member', split_axis=0, concat_axis=0, tiled=True)]
    unnamed x13 -> x15, local copies, waits for them, and re-layouts: 2.49 us -> 3.12 us
  transfers between devices with their start and end apart: 3 -> 5, of which waited for: 3 -> 5; matrix products, arithmetic and copies ran while one was open for 2% -> 2% of each run, Pallas kernels for 0% -> 10%
where the time goes in v2:
time: 111 us; the launch traced here: 110 us
  waiting for transfers between devices  42 us (38%)
  starting transfers between devices  25.6 us (23%)
  Pallas kernels  20.3 us (18%)
  blocking collectives  12.9 us (12%)
  local copies, waits for them, and re-layouts  4.81 us (4%)
  other arithmetic  3.02 us (3%)
    ppermute x1, waiting for transfers between devices, run(): back = lax.ppermute(result[:half], 'space', up)  18.5 us
    all_to_all x1, blocking collectives, mixed(): lax.all_to_all(chunk, 'member', split_axis=0, concat_axis=0, tiled=True)  12.9 us
    ppermute x1, starting transfers between devices, run(): other = lax.ppermute(own[:half], 'space', down)  12.5 us
    pallas_call x2, Pallas kernels, member_layer(): pl.pallas_call(member_kernel, grid=(count // block,), out_shape=jax.Shape...  10.9 us
    all_to_all x2, waiting for transfers between devices, mixed(): lax.all_to_all(points, 'member', split_axis=0, concat_axis=0, tiled=True)  10.6 us
    ppermute x1, waiting for transfers between devices, run(): other = lax.ppermute(own[:half], 'space', down)  9.69 us
    pallas_call x1, Pallas kernels, window_layer(): pl.pallas_call(window_kernel, grid=(longitudes // WIN,), out_shape=jax.Sh...  9.34 us
    all_to_all x2, starting transfers between devices, mixed(): lax.all_to_all(points, 'member', split_axis=0, concat_axis=0, tiled=True)  8.71 us
  transfers between devices with their start and end apart: 5, of which 5 were waited for; matrix products, arithmetic and copies ran while one was open for 2% of the time, Pallas kernels for 10%

profile of v2, /device:TPU:1, one launch (start us, length us, event | category | flops | bytes accessed | tf_op | source)
XLA Modules:
  0.0 109.7 jit_solution(12549979538599096490)
XLA Ops:
  0.0 0.0 copy-start.3
  0.0 0.0 copy-start.12
  0.0 0.6 copy-done.3
  0.7 0.6 fusion.2
  1.9 0.0 copy-start.22
  2.0 0.0 copy-start.23
  2.0 0.0 copy-start.24
  2.0 1.0 copy.18
  3.0 0.0 copy-start.21
  3.0 0.0 copy-done.12
  3.0 0.0 copy-done.22
  3.1 0.0 copy-done.23
  3.1 0.0 copy-done.24
  3.1 0.6 copy-done.21
  3.7 105.2 %conditional.1 = (bf16[1,16,64,256]{3,2,1,0:T(8,128)(2,1)S(1)}) conditional(s32[]{:T(128)} %convert_element_type.3, (s32[]{:T(128)}, s32[1]{0:T(128)}, s32[1]{0:T(128)}, bf16[16,64,256]{2,1,0:T(8,128)(2,1)}, f32[1,256]{1,0:T(1,128)S(1)}, /*index=5*/bf16[256,768]{1,0:T(8,128)(2,1)S(1)}, bf16[256,256]{1,0:T(8,128)(2,1)}, f32[1,256]{1,0:T(1,128)S(1)}, ...), branch_computations={%region_0.1_spmd, %region_1.2_spmd} | conditional | flops 7200524288 | bytes 35390072 | solution.py:290
  3.7 0.0 copy-start.1
  3.7 1.0 slice.36
  4.8 12.5 %collective-permute-start.2 = (bf16[8,64,256]{2,1,0:T(8,128)(2,1)S(1)}, bf16[8,64,256]{2,1,0:T(8,128)(2,1)S(1)}, u32[]{:S(2)}, u32[]{:S(2)}) collective-permute-start(bf16[8,64,256]{2,1,0:T(8,128)(2,1)S(1)} %slice.36), channel_id=1, source_target_pairs={{1,0},{2,1},{3,2},{4,3},{5,4},{6,5},{7,6},{8,7},{9,8},{10,9},{11,1... | collective-permute-start | bytes 786440 | tf_op jit(solution)/shard_map/cond/branch_1_fun/ppermute | solution.py:251
  17.2 0.7 compare_bitcast_fusion.1
  17.9 9.7 %collective-permute-done.2 = bf16[8,64,256]{2,1,0:T(8,128)(2,1)S(1)} collective-permute-done((bf16[8,64,256]{2,1,0:T(8,128)(2,1)S(1)}, bf16[8,64,256]{2,1,0:T(8,128)(2,1)S(1)}, u32[]{:S(2)}, u32[]{:S(2)}) %collective-permute-start.2) | collective-permute-done | bytes 262176 | tf_op jit(solution)/shard_map/cond/branch_1_fun/ppermute | solution.py:251
  27.6 0.0 copy-done.1
  27.6 0.0 copy-start.18
  27.6 0.8 fusion.1
  28.4 0.0 copy-start.5
  28.4 0.0 copy-start.7
  28.4 12.9 %all_to_all.33.x_ref = bf16[8,64,256]{2,1,0:T(8,128)(2,1)S(1)} all-to-all(bf16[8,64,256]{2,1,0:T(8,128)(2,1)S(1)} %get-tuple-element.130), channel_id=1, replica_groups=mesh['member'=8,'space'=32] {'member'}, dimensions={0} | all-to-all | bytes 524288 | tf_op jit(solution)/shard_map/cond/branch_1_fun/all_to_all | solution.py:263
  41.3 4.4 %all-to-all-start.4 = ((bf16[8,64,256]{2,1,0:T(8,128)(2,1)}), bf16[8,64,256]{2,1,0:T(8,128)(2,1)S(1)}, u32[]{:S(2)}, u32[]{:S(2)}) async-start(bf16[8,64,256]{2,1,0:T(8,128)(2,1)} %get-tuple-element.131), calls=%async_computation.4 | async-start | bytes 524288 | tf_op jit(solution)/shard_map/cond/branch_1_fun/all_to_all | solution.py:263
  45.7 0.0 copy-done.18
  45.7 0.0 copy-done.5
  45.7 0.0 copy-done.7
  45.7 5.5 %branch_1_fun.4 = bf16[8,64,256]{2,1,0:T(8,128)(2,1)} custom-call(bf16[8,64,256]{2,1,0:T(8,128)(2,1)S(1)} %all_to_all.33.x_ref, f32[1,256]{1,0:T(1,128)S(1)} %get-tuple-element.110.gain_ref, bf16[256,768]{1,0:T(8,128)(2,1)S(1)} %get-tuple-element.111.qkv_ref, bf16[256,256]{1,0:T(8,128)(2,1)S(1)} %copy-done.18, f32[1,256]{1,0:T(1,128)S(1)} %get-tuple-element.113.gain2_ref, ...), custom_call_target="tpu_custom_call" | custom-call | flops 1600000000 | bytes 3145728 | tf_op jit(solution)/shard_map/cond/branch_1_fun/pallas_call | solution.py:189
  51.2 3.2 %all-to-all-done.4.x_ref = bf16[8,64,256]{2,1,0:T(8,128)(2,1)S(1)} async-done(((bf16[8,64,256]{2,1,0:T(8,128)(2,1)}), bf16[8,64,256]{2,1,0:T(8,128)(2,1)S(1)}, u32[]{:S(2)}, u32[]{:S(2)}) %all-to-all-start.4) | async-done | bytes 262176 | tf_op jit(solution)/shard_map/cond/branch_1_fun/all_to_all | solution.py:263
  54.4 4.4 %all-to-all-start.7 = ((bf16[8,64,256]{2,1,0:T(8,128)(2,1)}), bf16[8,64,256]{2,1,0:T(8,128)(2,1)S(1)}, u32[]{:S(2)}, u32[]{:S(2)}) async-start(bf16[8,64,256]{2,1,0:T(8,128)(2,1)} %branch_1_fun.4), calls=%async_computation.7 | async-start | bytes 524288 | tf_op jit(solution)/shard_map/cond/branch_1_fun/all_to_all | solution.py:267
  58.8 5.5 %branch_1_fun.3 = bf16[8,64,256]{2,1,0:T(8,128)(2,1)} custom-call(bf16[8,64,256]{2,1,0:T(8,128)(2,1)S(1)} %all-to-all-done.4.x_ref, f32[1,256]{1,0:T(1,128)S(1)} %get-tuple-element.110.gain_ref, bf16[256,768]{1,0:T(8,128)(2,1)S(1)} %get-tuple-element.111.qkv_ref, bf16[256,256]{1,0:T(8,128)(2,1)S(1)} %copy-done.18, ...), custom_call_target="tpu_custom_call" | custom-call | flops 1600000000 | bytes 3145728 | tf_op jit(solution)/shard_map/cond/branch_1_fun/pallas_call | solution.py:189
  64.2 3.3 %all-to-all-done.7.high_ref = bf16[8,64,256]{2,1,0:T(8,128)(2,1)S(1)} async-done(((bf16[8,64,256]{2,1,0:T(8,128)(2,1)}), bf16[8,64,256]{2,1,0:T(8,128)(2,1)S(1)}, u32[]{:S(2)}, u32[]{:S(2)}) %all-to-all-start.7) | async-done | bytes 262176 | tf_op jit(solution)/shard_map/cond/branch_1_fun/all_to_all | solution.py:267
  67.5 4.4 %all-to-all-start.5 = ((bf16[8,64,256]{2,1,0:T(8,128)(2,1)}), bf16[8,64,256]{2,1,0:T(8,128)(2,1)S(1)}, u32[]{:S(2)}, u32[]{:S(2)}) async-start(bf16[8,64,256]{2,1,0:T(8,128)(2,1)} %branch_1_fun.3), calls=%async_computation.5 | async-start | bytes 524288 | tf_op jit(solution)/shard_map/cond/branch_1_fun/all_to_all | solution.py:267
  71.8 1.4 %pad_add_fusion.1.place_ref = s32[4]{0:T(128)S(1)} fusion(s32[1]{0:T(128)} %bitcast.6, s32[1]{0:T(128)} %bitcast.5, s32[1]{0:T(128)} %get-tuple-element.107, s32[1]{0:T(128)} %get-tuple-element.106), kind=kLoop, calls=%fused_computation.9 | loop fusion | flops 12 | bytes 32 | tf_op jit(solution)/shard_map/cond/branch_1_fun/stack | solution.py:260
  73.2 7.4 %all-to-all-done.5.low_ref = bf16[8,64,256]{2,1,0:T(8,128)(2,1)S(1)} async-done(((bf16[8,64,256]{2,1,0:T(8,128)(2,1)}), bf16[8,64,256]{2,1,0:T(8,128)(2,1)S(1)}, u32[]{:S(2)}, u32[]{:S(2)}) %all-to-all-start.5) | async-done | bytes 262176 | tf_op jit(solution)/shard_map/cond/branch_1_fun/all_to_all | solution.py:267
  80.6 0.0 copy-done.11
  80.6 0.0 copy-done.16
  80.6 0.0 copy-done.20
  80.6 0.0 copy-done.9
  80.6 9.3 %branch_1_fun.5 = bf16[16,64,256]{2,1,0:T(8,128)(2,1)S(1)} custom-call(s32[4]{0:T(128)S(1)} %pad_add_fusion.1.place_ref, bf16[8,64,256]{2,1,0:T(8,128)(2,1)S(1)} %all-to-all-done.5.low_ref, bf16[8,64,256]{2,1,0:T(8,128)(2,1)S(1)} %all-to-all-done.7.high_ref, s32[32,16,64]{2,1,0:T(8,128)S(1)} %get-tuple-element.116.kinds_ref, ...), custom_call_target="tpu_custom_call" | custom-call | flops 4000000000 | bytes 3145728 | tf_op jit(solution)/shard_map/cond/branch_1_fun/pallas_call | solution.py:205
  90.0 0.1 collective-permute-start.3
  90.0 18.5 %collective-permute-done.3 = bf16[8,64,256]{2,1,0:T(8,128)(2,1)S(1)} collective-permute-done((bf16[8,64,256]{2,1,0:T(8,128)(2,1)S(1)}, bf16[8,64,256]{2,1,0:T(8,128)(2,1)S(1)}, u32[]{:S(2)}, u32[]{:S(2)}) %collective-permute-start.3) | collective-permute-done | bytes 262176 | tf_op jit(solution)/shard_map/cond/branch_1_fun/ppermute | solution.py:283
  108.5 0.1 broadcast_select_fusion.2
  108.9 0.0 copy-start.2
  108.9 0.8 copy-done.2
  (8 shorter events, 0.1 us)
Async XLA Ops:
  0.0 0.7 copy-start.3
  0.0 3.0 %copy-start.12 = (bf16[256,768]{1,0:T(8,128)(2,1)S(1)}, bf16[256,768]{1,0:T(8,128)(2,1)}, u32[]{:S(2)}) copy-start(bf16[256,768]{1,0:T(8,128)(2,1)} %param.21) | copy-start | bytes 1179652
  1.9 1.1 %copy-start.22 = (f32[256]{0:T(256)S(1)}, f32[256]{0:T(256)}, u32[]{:S(2)}) copy-start(f32[256]{0:T(256)} %param.23) | copy-start | bytes 3076
  2.0 1.1 %copy-start.23 = (f32[256]{0:T(256)S(1)}, f32[256]{0:T(256)}, u32[]{:S(2)}) copy-start(f32[256]{0:T(256)} %param.26) | copy-start | bytes 3076
  2.0 1.1 %copy-start.24 = (f32[256]{0:T(256)S(1)}, f32[256]{0:T(256)}, u32[]{:S(2)}) copy-start(f32[256]{0:T(256)} %param.29) | copy-start | bytes 3076
  3.0 0.7 copy-start.21
  3.7 23.9 %copy-start.1 = (bf16[16,64,256]{2,1,0:T(8,128)(2,1)S(1)}, bf16[16,64,256]{2,1,0:T(8,128)(2,1)}, u32[]{:S(2)}) copy-start(bf16[16,64,256]{2,1,0:T(8,128)(2,1)} %get-tuple-element.109) | copy-start | bytes 1572868 | tf_op jit(solution)/shard_map/cond
  4.8 22.8 %collective-permute-start.2 = (bf16[8,64,256]{2,1,0:T(8,128)(2,1)S(1)}, bf16[8,64,256]{2,1,0:T(8,128)(2,1)S(1)}, u32[]{:S(2)}, u32[]{:S(2)}) collective-permute-start(bf16[8,64,256]{2,1,0:T(8,128)(2,1)S(1)} %slice.36), channel_id=1, source_target_pairs={{1,0},{2,1},{3,2},{4,3},{5,4},{6,5},{7,6},{8,7},{9,8},{10,9},{11,1... | collective-permute-start | bytes 786440 | tf_op jit(solution)/shard_map/cond/branch_1_fun/ppermute | solution.py:251
  27.6 18.1 %copy-start.18 = (bf16[256,256]{1,0:T(8,128)(2,1)S(1)}, bf16[256,256]{1,0:T(8,128)(2,1)}, u32[]{:S(2)}) copy-start(bf16[256,256]{1,0:T(8,128)(2,1)} %get-tuple-element.112.out_ref) | copy-start | bytes 393220 | tf_op jit(solution)/shard_map/cond
  28.4 17.3 %copy-start.5 = (bf16[256,1024]{1,0:T(8,128)(2,1)S(1)}, bf16[256,1024]{1,0:T(8,128)(2,1)}, u32[]{:S(2)}) copy-start(bf16[256,1024]{1,0:T(8,128)(2,1)} %get-tuple-element.114.in2_ref) | copy-start | bytes 1572868 | tf_op jit(solution)/shard_map/cond
  28.4 17.3 %copy-start.7 = (bf16[1024,256]{1,0:T(8,128)(2,1)S(1)}, bf16[1024,256]{1,0:T(8,128)(2,1)}, u32[]{:S(2)}) copy-start(bf16[1024,256]{1,0:T(8,128)(2,1)} %get-tuple-element.115.out2_ref) | copy-start | bytes 1572868 | tf_op jit(solution)/shard_map/cond
  41.3 13.1 %all-to-all-start.4 = ((bf16[8,64,256]{2,1,0:T(8,128)(2,1)}), bf16[8,64,256]{2,1,0:T(8,128)(2,1)S(1)}, u32[]{:S(2)}, u32[]{:S(2)}) async-start(bf16[8,64,256]{2,1,0:T(8,128)(2,1)} %get-tuple-element.131), calls=%async_computation.4 | async-start | bytes 524288 | tf_op jit(solution)/shard_map/cond/branch_1_fun/all_to_all | solution.py:263
  54.4 13.1 %all-to-all-start.7 = ((bf16[8,64,256]{2,1,0:T(8,128)(2,1)}), bf16[8,64,256]{2,1,0:T(8,128)(2,1)S(1)}, u32[]{:S(2)}, u32[]{:S(2)}) async-start(bf16[8,64,256]{2,1,0:T(8,128)(2,1)} %branch_1_fun.4), calls=%async_computation.7 | async-start | bytes 524288 | tf_op jit(solution)/shard_map/cond/branch_1_fun/all_to_all | solution.py:267
  58.7 21.8 %copy-start.11 = (bf16[1024,256]{1,0:T(8,128)(2,1)S(1)}, bf16[1024,256]{1,0:T(8,128)(2,1)}, u32[]{:S(2)}) copy-start(bf16[1024,256]{1,0:T(8,128)(2,1)} %get-tuple-element.122.out2_ref) | copy-start | bytes 1572868 | tf_op jit(solution)/shard_map/cond
  58.8 21.8 %copy-start.16 = (bf16[256,768]{1,0:T(8,128)(2,1)S(1)}, bf16[256,768]{1,0:T(8,128)(2,1)}, u32[]{:S(2)}) copy-start(bf16[256,768]{1,0:T(8,128)(2,1)} %get-tuple-element.118.qkv_ref) | copy-start | bytes 1179652 | tf_op jit(solution)/shard_map/cond
  58.8 21.8 %copy-start.20 = (bf16[256,256]{1,0:T(8,128)(2,1)S(1)}, bf16[256,256]{1,0:T(8,128)(2,1)}, u32[]{:S(2)}) copy-start(bf16[256,256]{1,0:T(8,128)(2,1)} %get-tuple-element.119.out_ref) | copy-start | bytes 393220 | tf_op jit(solution)/shard_map/cond
  64.2 16.4 %copy-start.9 = (bf16[256,1024]{1,0:T(8,128)(2,1)S(1)}, bf16[256,1024]{1,0:T(8,128)(2,1)}, u32[]{:S(2)}) copy-start(bf16[256,1024]{1,0:T(8,128)(2,1)} %get-tuple-element.121.in2_ref) | copy-start | bytes 1572868 | tf_op jit(solution)/shard_map/cond
  67.5 13.1 %all-to-all-start.5 = ((bf16[8,64,256]{2,1,0:T(8,128)(2,1)}), bf16[8,64,256]{2,1,0:T(8,128)(2,1)S(1)}, u32[]{:S(2)}, u32[]{:S(2)}) async-start(bf16[8,64,256]{2,1,0:T(8,128)(2,1)} %branch_1_fun.3), calls=%async_computation.5 | async-start | bytes 524288 | tf_op jit(solution)/shard_map/cond/branch_1_fun/all_to_all | solution.py:267
  90.0 18.6 %collective-permute-start.3 = (bf16[8,64,256]{2,1,0:T(8,128)(2,1)S(1)}, bf16[8,64,256]{2,1,0:T(8,128)(2,1)S(1)}, u32[]{:S(2)}, u32[]{:S(2)}) collective-permute-start(bf16[8,64,256]{2,1,0:T(8,128)(2,1)S(1)} %slice.46), channel_id=1, source_target_pairs={{0,1},{1,2},{2,3},{3,4},{4,5},{5,6},{6,7},{7,8},{8,9},{9,10},{10,1... | collective-permute-start | bytes 786440 | tf_op jit(solution)/shard_map/cond/branch_1_fun/ppermute | solution.py:283
  108.9 0.8 copy-start.2

commit v3 on v1

v3 whole, which is shorter than its diff:
```python
import math

import jax
import jax.numpy as jnp
from jax import lax
from jax.experimental import pallas as pl
from jax.experimental.pallas import tpu as pltpu
from jax.sharding import PartitionSpec as P

HEADS = 8
WIN = 16
EPSILON = 1e-05
BLOCK = 256
FAR = 1e30
VMEM = pl.BlockSpec(memory_space=pltpu.VMEM)
SMEM = pl.BlockSpec(memory_space=pltpu.SMEM)


def normalise(values, gains):
    center = jnp.mean(values, axis=-1, keepdims=True)
    shifted = values - center
    spread = jnp.mean(shifted * shifted, axis=-1, keepdims=True)
    return (shifted * lax.rsqrt(spread + EPSILON) * gains).astype(jnp.bfloat16)


def wide_dot(a, b):
    return jnp.dot(a, b, preferred_element_type=jnp.float32)


def twice_gelu(x):
    inner = x * (0.7978845608028654 + 0.035677408136300125 * (x * x))
    return (x + x * jnp.tanh(inner)).astype(jnp.bfloat16)


def feed_forward(stream, gain_ref, in_ref, out_ref):
    wide = stream.astype(jnp.float32)
    normed = normalise(wide, gain_ref[...])
    hidden_size = in_ref.shape[1]
    update = None
    for start in range(0, hidden_size, BLOCK):
        hidden = twice_gelu(wide_dot(normed, in_ref[:, start : start + BLOCK]))
        part = wide_dot(hidden, out_ref[start : start + BLOCK, :])
        update = part if update is None else update + part
    return (wide + 0.5 * update).astype(jnp.bfloat16)


def mix_members(x, gain_ref, qkv_ref, out_ref, gain2_ref, in2_ref, out2_ref):
    members, points, features = x.shape
    tokens = members * points
    size = features // HEADS
    stream = x.reshape(tokens, features).astype(jnp.float32)
    normed = normalise(stream, gain_ref[...])
    query = wide_dot(normed, qkv_ref[:, :features]) * (math.log2(math.e) / math.sqrt(size))
    key = wide_dot(normed, qkv_ref[:, features : 2 * features]).astype(jnp.bfloat16)
    value = wide_dot(normed, qkv_ref[:, 2 * features :])
    query = query.astype(jnp.bfloat16).reshape(members, points, features)
    key = key.reshape(members, points, features)
    value = value.astype(jnp.bfloat16).astype(jnp.float32).reshape(members, points, features)

    lane = lax.broadcasted_iota(jnp.int32, (features, 128), 1) % 64
    head = lax.broadcasted_iota(jnp.int32, (features, 128), 0) // size
    place = lane - head
    scores = jnp.zeros((tokens, 128), jnp.float32)
    for j in range(members):
        pick = jnp.where((place == j * HEADS) & (lane // HEADS == j), 1.0, 0.0).astype(jnp.bfloat16)
        product = (query * key[j][None]).reshape(tokens, features)
        scores = scores + wide_dot(product, pick)
    top = scores
    for step in (8, 16, 32):
        top = jnp.maximum(top, pltpu.roll(top, step, 1))
    weights = jnp.exp2(scores - top)
    total = weights
    for step in (8, 16, 32):
        total = total + pltpu.roll(total, step, 1)
    weights = (weights / total).astype(jnp.bfloat16)

    lane = lax.broadcasted_iota(jnp.int32, (128, features), 0)
    head = lax.broadcasted_iota(jnp.int32, (128, features), 1) // size
    place = lane - head
    mixed = None
    for j in range(members):
        spread = jnp.where(place == j * HEADS, 1.0, 0.0).astype(jnp.bfloat16)
        widened = wide_dot(weights, spread).reshape(members, points, features)
        part = widened * value[j][None]
        mixed = part if mixed is None else mixed + part
    mixed = mixed.reshape(tokens, features).astype(jnp.bfloat16)
    stream = (stream + wide_dot(mixed, out_ref[...])).astype(jnp.bfloat16)
    result = feed_forward(stream, gain2_ref, in2_ref, out2_ref)
    return result.reshape(members, points, features)


def first_member_kernel(x_ref, *refs):
    *params, o_ref = refs
    o_ref[...] = mix_members(x_ref[...], *params)


def second_member_kernel(slot, x_ref, done_ref, *refs):
    *params, o_ref = refs
    o_ref[:, 1 - slot] = done_ref[...]
    o_ref[:, slot] = mix_members(x_ref[...], *params)


def merging_kernel(first_row, shifts_ref, later_ref, earlier_ref, o_ref):
    for i in range(o_ref.shape[0]):
        o_ref[i] = jnp.where(first_row + i >= shifts_ref[0], later_ref[i], earlier_ref[i])


def window_kernel(
    window_below,
    shifts_ref,
    x_ref,
    kinds_ref,
    gain_ref,
    qkv_ref,
    out_ref,
    gain2_ref,
    in2_ref,
    out2_ref,
    low_ref,
    high_ref,
    kinds_scratch,
    sems,
):
    half, longitudes, features = low_ref.shape
    windows = longitudes // WIN
    size = features // HEADS
    group_lanes = features // 2
    tokens = WIN * WIN
    lat_shift, lon_shift = shifts_ref[0], shifts_ref[1]
    space = lax.axis_index("space")
    spaces = kinds_ref.shape[0] // WIN
    if window_below:
        blocks = (space, lax.rem(space + 1, spaces))
    else:
        blocks = (lax.rem(space + spaces - 1, spaces), space)
    copies = [
        pltpu.make_async_copy(
            kinds_ref.at[pl.ds(pl.multiple_of(block * WIN, WIN), WIN)],
            kinds_scratch.at[n],
            sems.at[n],
        )
        for n, block in enumerate(blocks)
    ]
    for copy in copies:
        copy.start()

    column = lax.broadcasted_iota(jnp.int32, (WIN, WIN, features), 1)
    inside = column >= lon_shift
    tiles = [
        jnp.concatenate(
            [x_ref[:, part, w * WIN : (w + 1) * WIN, :] for part in range(2)]
        ).astype(jnp.float32)
        for w in range(windows)
    ]
    stream = jnp.concatenate(
        [
            jnp.where(inside, tiles[w], tiles[(w + 1) % windows]).reshape(tokens, features)
            for w in range(windows)
        ]
    )
    normed = normalise(stream, gain_ref[...])
    query = wide_dot(normed, qkv_ref[:, :features]) * (math.log2(math.e) / math.sqrt(size))
    query = query.astype(jnp.bfloat16)
    key = wide_dot(normed, qkv_ref[:, features : 2 * features])
    value = wide_dot(normed, qkv_ref[:, 2 * features :]).astype(jnp.bfloat16)

    for copy in copies:
        copy.wait()
    row = lax.broadcasted_iota(jnp.int32, (WIN, longitudes), 0)
    kinds = jnp.where(row >= lat_shift, kinds_scratch[0], kinds_scratch[1]).astype(jnp.float32)
    kinds = jnp.broadcast_to(kinds[:, None, :], (WIN, WIN, longitudes))
    kind_column = lax.broadcasted_iota(jnp.int32, (WIN, WIN, longitudes), 1)
    kind_lane = lax.broadcasted_iota(jnp.int32, (WIN, WIN, longitudes), 2)

    lane = lax.broadcasted_iota(jnp.int32, (tokens, features), 1)
    lane_row = lax.broadcasted_iota(jnp.int32, (1, features), 1)

    def head_lanes(first):
        return jnp.where(
            (lane_row >= first) & (lane_row < first + size), 1.0, 0.0
        ).astype(jnp.bfloat16)

    attended = []
    for w in range(windows):
        at = slice(w * tokens, (w + 1) * tokens)
        wanted = kind_column + jnp.where(
            kind_column >= lon_shift, w * WIN, (w + 1) % windows * WIN
        )
        kind = jnp.where(kind_lane == wanted, kinds, 0.0).reshape(tokens, longitudes)
        kind = jnp.sum(kind, axis=-1, keepdims=True)
        halves = []
        for group in range(2):
            first = features - size if group == 0 else 0
            query_marks = jnp.where(
                lane == first, -FAR * kind, jnp.where(lane == first + 1, -FAR * (1.0 - kind), 0.0)
            ).astype(jnp.bfloat16)
            marked = jnp.where(lane == first, 1.0 - kind, jnp.where(lane == first + 1, kind, 0.0))
            free = (lane >= first) & (lane < first + size)
            keys = jnp.where(free, marked, key[at]).astype(jnp.bfloat16)
            total = None
            for h in range(group * HEADS // 2, (group + 1) * HEADS // 2):
                q = query[at] * head_lanes(h * size) + query_marks
                scores = lax.dot_general(
                    q, keys, (((1,), (1,)), ((), ())), preferred_element_type=jnp.float32
                )
                top = jnp.max(scores, axis=-1, keepdims=True)
                weights = jnp.exp2(scores - top).astype(jnp.bfloat16)
                opposite = h * size + (group_lanes if group == 0 else -group_lanes)
                v = value[at] * head_lanes(h * size) + head_lanes(opposite)
                part = wide_dot(weights, v)
                total = part if total is None else total + part
            if group == 0:
                halves.append(total[:, :group_lanes] / total[:, group_lanes:])
            else:
                halves.append(total[:, group_lanes:] / total[:, :group_lanes])
        attended.append(jnp.concatenate(halves, axis=-1).astype(jnp.bfloat16))
    attended = jnp.concatenate(attended)
    stream = (stream + wide_dot(attended, out_ref[...])).astype(jnp.bfloat16)
    result = feed_forward(stream, gain2_ref, in2_ref, out2_ref).astype(jnp.float32)
    result = result.reshape(windows, WIN, WIN, features)
    for w in range(windows):
        tile = jnp.where(inside, result[w], result[(w + windows - 1) % windows])
        tile = tile.astype(jnp.bfloat16)
        low_ref[:, w * WIN : (w + 1) * WIN, :] = tile[:half]
        high_ref[:, w * WIN : (w + 1) * WIN, :] = tile[half:]


def cost(tokens, flops_per_token):
    return pl.CostEstimate(
        flops=tokens * flops_per_token, bytes_accessed=3 * 2**20, transcendentals=tokens * 2048
    )


LARGE = pltpu.CompilerParams(vmem_limit_bytes=48 * 2**20)


def first_member_layer(points, *params):
    return pl.pallas_call(
        first_member_kernel,
        out_shape=jax.ShapeDtypeStruct(points.shape, jnp.bfloat16),
        in_specs=[VMEM] * (1 + len(params)),
        out_specs=VMEM,
        compiler_params=LARGE,
        cost_estimate=cost(512, 1600000),
    )(points, *params)


def second_member_layer(slot, points, done, *params):
    members, *rest = points.shape

    def kernel(*refs):
        second_member_kernel(slot, *refs)

    return pl.pallas_call(
        kernel,
        out_shape=jax.ShapeDtypeStruct((members, 2, *rest), jnp.bfloat16),
        in_specs=[VMEM] * (2 + len(params)),
        out_specs=VMEM,
        compiler_params=LARGE,
        cost_estimate=cost(512, 1600000),
    )(points, done, *params)


def merge_rows(first_row, shifts, later, earlier):
    def kernel(*refs):
        merging_kernel(first_row, *refs)

    return pl.pallas_call(
        kernel,
        out_shape=jax.ShapeDtypeStruct(later.shape, jnp.bfloat16),
        in_specs=[SMEM, VMEM, VMEM],
        out_specs=VMEM,
    )(shifts, later, earlier)


def window_layer(window_below, shifts, region, kinds, *params):
    half, _, longitudes, features = region.shape

    def kernel(*refs):
        window_kernel(window_below, *refs)

    return pl.pallas_call(
        kernel,
        out_shape=[jax.ShapeDtypeStruct((half, longitudes, features), jnp.bfloat16)] * 2,
        in_specs=[SMEM, VMEM, pl.BlockSpec(memory_space=pl.ANY)] + [VMEM] * len(params),
        out_specs=[VMEM] * 2,
        scratch_shapes=[
            pltpu.VMEM((2, WIN, longitudes), jnp.int32),
            pltpu.SemaphoreType.DMA((2,)),
        ],
        compiler_params=LARGE,
        cost_estimate=cost(1024, 2000000),
    )(shifts, region, kinds, *params)


def on_device(
    ensemble,
    shifts,
    land_sea,
    member_gain,
    member_qkv,
    member_out,
    first_gain,
    first_in,
    first_out,
    window_gain,
    window_qkv,
    window_out,
    second_gain,
    second_in,
    second_out,
):
    _, rows, longitudes, features = ensemble.shape
    half = rows // 2
    spaces = lax.axis_size("space")
    up = [(i, (i + 1) % spaces) for i in range(spaces)]
    down = [(j, i) for i, j in up]
    gains = [g.reshape(1, features) for g in (member_gain, first_gain, window_gain, second_gain)]
    members_first = (gains[0], member_qkv, member_out, gains[1], first_in, first_out)
    windows_second = (gains[2], window_qkv, window_out, gains[3], second_in, second_out)

    def exchange(parts):
        return lax.all_to_all(parts, "member", split_axis=0, concat_axis=0, tiled=True)

    def run(window_below):
        low, high = lax.optimization_barrier((ensemble[0, :half], ensemble[0, half:]))
        settled, open_half = (high, low) if window_below else (low, high)
        other = lax.ppermute(open_half, "space", down if window_below else up)
        first = exchange(settled)
        if window_below:
            merged = merge_rows(0, shifts, open_half, other)
        else:
            merged = merge_rows(half, shifts, other, open_half)
        second = exchange(merged)
        first = first_member_layer(first, *members_first)
        mixed = second_member_layer(0 if window_below else 1, second, first, *members_first)
        region = exchange(mixed)
        low, high = window_layer(window_below, shifts, region, land_sea, *windows_second)
        if window_below:
            back = lax.ppermute(low, "space", up)
            return jnp.concatenate([merge_rows(0, shifts, low, back), high])
        back = lax.ppermute(high, "space", down)
        return jnp.concatenate([low, merge_rows(half, shifts, back, high)])

    out = lax.cond(shifts[0] <= half, lambda: run(True), lambda: run(False))
    return out[None]


def solution(mesh):
    return jax.shard_map(
        on_device,
        mesh=mesh,
        in_specs=(P("member", "space", None, None),) + (P(),) * 14,
        out_specs=P("member", "space", None, None),
        check_vma=False,
    )
```

time: 105 us -> 102 us (0.971)
  the two profiles are of different devices: /device:TPU:1 before, /device:TPU:30 now
where the time goes in v3:
time: 102 us; the launch traced here: 101 us
  waiting for transfers between devices  56.4 us (55%)
  Pallas kernels  19.8 us (19%)
  starting transfers between devices  17.7 us (17%)
  local copies, waits for them, and re-layouts  5.47 us (5%)
    all_to_all x3, waiting for transfers between devices, exchange(): lax.all_to_all(parts, 'member', split_axis=0, concat_axis=0, tiled=True)  26.2 us
    ppermute x1, waiting for transfers between devices, run(): back = lax.ppermute(high, 'space', down)  22.2 us
    all_to_all x3, starting transfers between devices, exchange(): lax.all_to_all(parts, 'member', split_axis=0, concat_axis=0, tiled=True)  13.2 us
    ppermute x1, waiting for transfers between devices, run(): other = lax.ppermute(open_half, 'space', down if window_below else up)  7.94 us
    pallas_call x1, Pallas kernels, window_layer(): pl.pallas_call(kernel, out_shape=[jax.ShapeDtypeStruct((half, longitudes,...  6.49 us
    pallas_call x1, Pallas kernels, second_member_layer(): pl.pallas_call(kernel, out_shape=jax.ShapeDtypeStruct((members, 2, *rest)...  5.25 us
    pallas_call x1, Pallas kernels, first_member_layer(): pl.pallas_call(first_member_kernel, out_shape=jax.ShapeDtypeStruct(points...  4.47 us
    ppermute x1, starting transfers between devices, run(): other = lax.ppermute(open_half, 'space', down if window_below else up)  4.36 us
  transfers between devices with their start and end apart: 5, of which 5 were waited for; matrix products, arithmetic and copies ran while one was open for 0% of the time, Pallas kernels for 6%

profile of v3, /device:TPU:30, one launch (start us, length us, event | category | flops | bytes accessed | tf_op | source)
XLA Modules:
  0.0 101.1 jit_solution(13639908807489255437)
XLA Ops:
  0.0 0.0 copy-start.11
  0.0 0.7 copy-done.11
  0.7 0.0 copy-start.31
  0.7 0.0 copy-start.29
  0.7 0.0 copy-start.30
  0.7 0.0 copy-start.28
  0.7 0.6 copy-done.31
  1.4 0.0 copy-done.29
  1.4 0.0 copy-done.30
  1.4 0.0 copy-done.28
  1.4 98.9 %conditional.1 = (bf16[1,16,64,256]{3,2,1,0:T(8,128)(2,1)S(1)}) conditional(s32[]{:T(128)} %bitcast.6, (bf16[1,16,64,256]{3,2,1,0:T(8,128)(2,1)}, s32[2]{0:T(128)S(1)}, f32[1,256]{1,0:T(1,128)S(1)}, bf16[256,768]{1,0:T(8,128)(2,1)}, bf16[256,256]{1,0:T(8,128)(2,1)}, /*index=5*/f32[1,256]{1,0:T(1,128)S(1)}, bf16[256,1024]{1,0:T(8,128)(2,1)}, ...), branch_computations={%region_0.0_spmd, %region_1.0_spmd} | conditional | flops 3686662144 | bytes 34341412 | solution.py:345
  1.4 1.8 %slice_bitcast_fusion = (bf16[8,64,256]{2,1,0:T(8,128)(2,1)S(1)}, bf16[8,64,256]{2,1,0:T(8,128)(2,1)}) fusion(bf16[1,16,64,256]{3,2,1,0:T(8,128)(2,1)} %get-tuple-element.70), kind=kLoop, calls=%fused_computation.1 | loop fusion | bytes 1048576 | tf_op jit(solution)/shard_map/cond/branch_0_fun/squeeze | solution.py:326
  3.2 0.0 copy-start.2
  3.2 0.0 copy-start.20
  3.2 6.0 %all-to-all-start.1 = ((bf16[8,64,256]{2,1,0:T(8,128)(2,1)}), bf16[8,64,256]{2,1,0:T(8,128)(2,1)S(1)}, u32[]{:S(2)}, u32[]{:S(2)}) async-start(bf16[8,64,256]{2,1,0:T(8,128)(2,1)} %get-tuple-element.72), calls=%async_computation.1 | async-start | bytes 524288 | tf_op jit(solution)/shard_map/cond/branch_0_fun/all_to_all | solution.py:323
  9.2 0.0 copy-done.2
  9.2 4.4 %collective-permute-start = (bf16[8,64,256]{2,1,0:T(8,128)(2,1)S(1)}, bf16[8,64,256]{2,1,0:T(8,128)(2,1)S(1)}, u32[]{:S(2)}, u32[]{:S(2)}) collective-permute-start(bf16[8,64,256]{2,1,0:T(8,128)(2,1)S(1)} %get-tuple-element.71.refs_2_), channel_id=1, source_target_pairs={{0,1},{1,2},{2,3},{3,4},{4,5},{5,6},{6,7},{7,8},{8,9},{9,10},{10,1... | collective-permute-start | bytes 786440 | tf_op jit(solution)/shard_map/cond/branch_0_fun/ppermute | solution.py:328
  13.6 7.9 %collective-permute-done.refs_1_ = bf16[8,64,256]{2,1,0:T(8,128)(2,1)S(1)} collective-permute-done((bf16[8,64,256]{2,1,0:T(8,128)(2,1)S(1)}, bf16[8,64,256]{2,1,0:T(8,128)(2,1)S(1)}, u32[]{:S(2)}, u32[]{:S(2)}) %collective-permute-start) | collective-permute-done | bytes 262176 | tf_op jit(solution)/shard_map/cond/branch_0_fun/ppermute | solution.py:328
  21.6 0.7 copy-done.7
  22.3 1.9 %branch_0_fun.5 = bf16[8,64,256]{2,1,0:T(8,128)(2,1)} custom-call(s32[2]{0:T(128)S(1)} %get-tuple-element.69.refs_0_, bf16[8,64,256]{2,1,0:T(8,128)(2,1)} %copy-done.7, bf16[8,64,256]{2,1,0:T(8,128)(2,1)} %copy-done.2), custom_call_target="tpu_custom_call" | custom-call | tf_op jit(solution)/shard_map/cond/branch_0_fun/pallas_call | solution.py:268
  24.1 6.2 %all-to-all-done.1.x_ref = bf16[8,64,256]{2,1,0:T(8,128)(2,1)S(1)} async-done(((bf16[8,64,256]{2,1,0:T(8,128)(2,1)}), bf16[8,64,256]{2,1,0:T(8,128)(2,1)S(1)}, u32[]{:S(2)}, u32[]{:S(2)}) %all-to-all-start.1) | async-done | bytes 262176 | tf_op jit(solution)/shard_map/cond/branch_0_fun/all_to_all | solution.py:323
  30.3 3.4 %all-to-all-start = ((bf16[8,64,256]{2,1,0:T(8,128)(2,1)}), bf16[8,64,256]{2,1,0:T(8,128)(2,1)S(1)}, u32[]{:S(2)}, u32[]{:S(2)}) async-start(bf16[8,64,256]{2,1,0:T(8,128)(2,1)} %branch_0_fun.5), calls=%async_computation | async-start | bytes 524288 | tf_op jit(solution)/shard_map/cond/branch_0_fun/all_to_all | solution.py:323
  33.7 0.0 copy-done.20
  33.7 0.0 copy-done.12
  33.7 0.0 copy-done.14
  33.7 0.0 copy-done.24
  33.7 4.5 %branch_0_fun.6.refs_1_ = bf16[8,64,256]{2,1,0:T(8,128)(2,1)S(1)} custom-call(bf16[8,64,256]{2,1,0:T(8,128)(2,1)S(1)} %all-to-all-done.1.x_ref, f32[1,256]{1,0:T(1,128)S(1)} %get-tuple-element.73.refs_0_.refs_2_, bf16[256,768]{1,0:T(8,128)(2,1)S(1)} %copy-done.20, bf16[256,256]{1,0:T(8,128)(2,1)S(1)} %copy-done.24, ...), custom_call_target="tpu_custom_call" | custom-call | flops 819200000 | bytes 3145728 | tf_op jit(solution)/shard_map/cond/branch_0_fun/pallas_call | solution.py:238
  38.2 5.1 %all-to-all-done.refs_0_ = bf16[8,64,256]{2,1,0:T(8,128)(2,1)S(1)} async-done(((bf16[8,64,256]{2,1,0:T(8,128)(2,1)}), bf16[8,64,256]{2,1,0:T(8,128)(2,1)S(1)}, u32[]{:S(2)}, u32[]{:S(2)}) %all-to-all-start) | async-done | bytes 262176 | tf_op jit(solution)/shard_map/cond/branch_0_fun/all_to_all | solution.py:323
  43.3 5.3 %branch_0_fun.7 = bf16[8,2,64,256]{3,2,1,0:T(8,128)(2,1)} custom-call(bf16[8,64,256]{2,1,0:T(8,128)(2,1)S(1)} %all-to-all-done.refs_0_, bf16[8,64,256]{2,1,0:T(8,128)(2,1)S(1)} %branch_0_fun.6.refs_1_, f32[1,256]{1,0:T(1,128)S(1)} %get-tuple-element.73.refs_0_.refs_2_, bf16[256,768]{1,0:T(8,128)(2,1)S(1)} %copy-done.20, bf16[256,256]{1,0:T(8,128)(2,1)S(1)} %copy-done.24, ...), custom_call_target="tpu_custom_call" | custom-call | flops 819200000 | bytes 3145728 | tf_op jit(solution)/shard_map/cond/branch_0_fun/pallas_call | solution.py:254
  48.6 3.8 %all-to-all-start.2 = ((bf16[8,2,64,256]{3,2,1,0:T(8,128)(2,1)}), bf16[8,2,64,256]{3,2,1,0:T(8,128)(2,1)S(1)}, u32[]{:S(2)}, u32[]{:S(2)}) async-start(bf16[8,2,64,256]{3,2,1,0:T(8,128)(2,1)} %branch_0_fun.7), calls=%async_computation.2 | async-start | bytes 1048576 | tf_op jit(solution)/shard_map/cond/branch_0_fun/all_to_all | solution.py:323
  52.4 0.0 copy-done.4
  52.4 0.0 copy-start.26
  52.4 0.1 copy.18.refs_2_
  52.6 14.9 %all-to-all-done.2.refs_1_ = bf16[8,2,64,256]{3,2,1,0:T(8,128)(2,1)S(1)} async-done(((bf16[8,2,64,256]{3,2,1,0:T(8,128)(2,1)}), bf16[8,2,64,256]{3,2,1,0:T(8,128)(2,1)S(1)}, u32[]{:S(2)}, u32[]{:S(2)}) %all-to-all-start.2) | async-done | bytes 524320 | tf_op jit(solution)/shard_map/cond/branch_0_fun/all_to_all | solution.py:323
  67.5 0.0 copy-done.22
  67.5 0.0 copy-done.16
  67.5 0.0 copy-done.18
  67.5 0.0 copy-done.26
  67.5 6.5 %branch_0_fun.8 = (bf16[8,64,256]{2,1,0:T(8,128)(2,1)S(1)}, bf16[8,64,256]{2,1,0:T(8,128)(2,1)S(1)}) custom-call(s32[2]{0:T(128)S(1)} %get-tuple-element.69.refs_0_, bf16[8,2,64,256]{3,2,1,0:T(8,128)(2,1)S(1)} %all-to-all-done.2.refs_1_, s32[512,64]{1,0:T(8,128)S(1)} %copy.18.refs_2_, f32[1,256]{1,0:T(1,128)S(1)} %get-tuple-element.80.refs_3_, ...), custom_call_target="tpu_custom_call" | custom-call | flops 2048000000 | bytes 3145728 | tf_op jit(solution)/shard_map/cond/branch_0_fun/pallas_call | solution.py:282
  74.0 0.0 copy-start
  74.0 0.1 collective-permute-start.1
  74.1 22.2 %collective-permute-done.1.refs_1_ = bf16[8,64,256]{2,1,0:T(8,128)(2,1)S(1)} collective-permute-done((bf16[8,64,256]{2,1,0:T(8,128)(2,1)S(1)}, bf16[8,64,256]{2,1,0:T(8,128)(2,1)S(1)}, u32[]{:S(2)}, u32[]{:S(2)}) %collective-permute-start.1) | collective-permute-done | bytes 262176 | tf_op jit(solution)/shard_map/cond/branch_0_fun/ppermute | solution.py:342
  96.3 0.0 copy-done
  96.3 0.7 copy-done.8
  97.0 1.8 %branch_0_fun.9 = bf16[8,64,256]{2,1,0:T(8,128)(2,1)} custom-call(s32[2]{0:T(128)S(1)} %get-tuple-element.69.refs_0_, bf16[8,64,256]{2,1,0:T(8,128)(2,1)} %copy-done.8, bf16[8,64,256]{2,1,0:T(8,128)(2,1)} %copy-done), custom_call_target="tpu_custom_call" | custom-call | tf_op jit(solution)/shard_map/cond/branch_0_fun/pallas_call | solution.py:268
  98.8 1.0 maximum_bitcast_fusion
  100.3 0.0 copy-start.6
  100.3 0.8 copy-done.6
  (9 shorter events, 0.0 us)
Async XLA Ops:
  0.0 0.7 copy-start.11
  0.7 0.7 copy-start.31
  0.7 0.7 copy-start.29
  0.7 0.7 copy-start.30
  0.7 0.7 copy-start.28
  3.2 6.0 %copy-start.2 = (bf16[8,64,256]{2,1,0:T(8,128)(2,1)}, bf16[8,64,256]{2,1,0:T(8,128)(2,1)S(1)}, u32[]{:S(2)}) copy-start(bf16[8,64,256]{2,1,0:T(8,128)(2,1)S(1)} %get-tuple-element.71.refs_2_) | copy-start | bytes 786436 | tf_op jit(solution)/shard_map/cond
  3.2 30.5 %copy-start.20 = (bf16[256,768]{1,0:T(8,128)(2,1)S(1)}, bf16[256,768]{1,0:T(8,128)(2,1)}, u32[]{:S(2)}) copy-start(bf16[256,768]{1,0:T(8,128)(2,1)} %get-tuple-element.74.refs_1_.refs_3_) | copy-start | bytes 1179652 | tf_op jit(solution)/shard_map/cond
  3.2 27.1 %all-to-all-start.1 = ((bf16[8,64,256]{2,1,0:T(8,128)(2,1)}), bf16[8,64,256]{2,1,0:T(8,128)(2,1)S(1)}, u32[]{:S(2)}, u32[]{:S(2)}) async-start(bf16[8,64,256]{2,1,0:T(8,128)(2,1)} %get-tuple-element.72), calls=%async_computation.1 | async-start | bytes 524288 | tf_op jit(solution)/shard_map/cond/branch_0_fun/all_to_all | solution.py:323
  9.2 12.3 %collective-permute-start = (bf16[8,64,256]{2,1,0:T(8,128)(2,1)S(1)}, bf16[8,64,256]{2,1,0:T(8,128)(2,1)S(1)}, u32[]{:S(2)}, u32[]{:S(2)}) collective-permute-start(bf16[8,64,256]{2,1,0:T(8,128)(2,1)S(1)} %get-tuple-element.71.refs_2_), channel_id=1, source_target_pairs={{0,1},{1,2},{2,3},{3,4},{4,5},{5,6},{6,7},{7,8},{8,9},{9,10},{10,1... | collective-permute-start | bytes 786440 | tf_op jit(solution)/shard_map/cond/branch_0_fun/ppermute | solution.py:328
  21.5 0.7 copy-start.7
  22.2 11.4 %copy-start.12 = (bf16[256,1024]{1,0:T(8,128)(2,1)S(1)}, bf16[256,1024]{1,0:T(8,128)(2,1)}, u32[]{:S(2)}) copy-start(bf16[256,1024]{1,0:T(8,128)(2,1)} %get-tuple-element.77.refs_4_.refs_6_) | copy-start | bytes 1572868 | tf_op jit(solution)/shard_map/cond
  22.2 11.4 %copy-start.14 = (bf16[1024,256]{1,0:T(8,128)(2,1)S(1)}, bf16[1024,256]{1,0:T(8,128)(2,1)}, u32[]{:S(2)}) copy-start(bf16[1024,256]{1,0:T(8,128)(2,1)} %get-tuple-element.78.refs_5_.refs_7_) | copy-start | bytes 1572868 | tf_op jit(solution)/shard_map/cond
  24.1 9.6 %copy-start.24 = (bf16[256,256]{1,0:T(8,128)(2,1)S(1)}, bf16[256,256]{1,0:T(8,128)(2,1)}, u32[]{:S(2)}) copy-start(bf16[256,256]{1,0:T(8,128)(2,1)} %get-tuple-element.75.refs_2_.refs_4_) | copy-start | bytes 393220 | tf_op jit(solution)/shard_map/cond
  30.3 13.1 %all-to-all-start = ((bf16[8,64,256]{2,1,0:T(8,128)(2,1)}), bf16[8,64,256]{2,1,0:T(8,128)(2,1)S(1)}, u32[]{:S(2)}, u32[]{:S(2)}) async-start(bf16[8,64,256]{2,1,0:T(8,128)(2,1)} %branch_0_fun.5), calls=%async_computation | async-start | bytes 524288 | tf_op jit(solution)/shard_map/cond/branch_0_fun/all_to_all | solution.py:323
  43.3 24.2 %copy-start.22 = (bf16[256,768]{1,0:T(8,128)(2,1)S(1)}, bf16[256,768]{1,0:T(8,128)(2,1)}, u32[]{:S(2)}) copy-start(bf16[256,768]{1,0:T(8,128)(2,1)} %get-tuple-element.81.refs_4_) | copy-start | bytes 1179652 | tf_op jit(solution)/shard_map/cond
  48.6 3.8 %copy-start.4 = (s32[512,64]{0,1:T(8,128)S(1)}, s32[512,64]{0,1:T(8,128)}, u32[]{:S(2)}) copy-start(s32[512,64]{0,1:T(8,128)} %get-tuple-element.116) | copy-start | bytes 393220 | tf_op jit(solution)/shard_map/cond
  48.6 18.9 %copy-start.16 = (bf16[256,1024]{1,0:T(8,128)(2,1)S(1)}, bf16[256,1024]{1,0:T(8,128)(2,1)}, u32[]{:S(2)}) copy-start(bf16[256,1024]{1,0:T(8,128)(2,1)} %get-tuple-element.84.refs_7_) | copy-start | bytes 1572868 | tf_op jit(solution)/shard_map/cond
  48.6 18.9 %copy-start.18 = (bf16[1024,256]{1,0:T(8,128)(2,1)S(1)}, bf16[1024,256]{1,0:T(8,128)(2,1)}, u32[]{:S(2)}) copy-start(bf16[1024,256]{1,0:T(8,128)(2,1)} %get-tuple-element.85.refs_8_) | copy-start | bytes 1572868 | tf_op jit(solution)/shard_map/cond
  48.6 18.9 %all-to-all-start.2 = ((bf16[8,2,64,256]{3,2,1,0:T(8,128)(2,1)}), bf16[8,2,64,256]{3,2,1,0:T(8,128)(2,1)S(1)}, u32[]{:S(2)}, u32[]{:S(2)}) async-start(bf16[8,2,64,256]{3,2,1,0:T(8,128)(2,1)} %branch_0_fun.7), calls=%async_computation.2 | async-start | bytes 1048576 | tf_op jit(solution)/shard_map/cond/branch_0_fun/all_to_all | solution.py:323
  52.4 15.1 %copy-start.26 = (bf16[256,256]{1,0:T(8,128)(2,1)S(1)}, bf16[256,256]{1,0:T(8,128)(2,1)}, u32[]{:S(2)}) copy-start(bf16[256,256]{1,0:T(8,128)(2,1)} %get-tuple-element.82.refs_5_) | copy-start | bytes 393220 | tf_op jit(solution)/shard_map/cond
  74.0 22.3 %copy-start = (bf16[8,64,256]{2,1,0:T(8,128)(2,1)}, bf16[8,64,256]{2,1,0:T(8,128)(2,1)S(1)}, u32[]{:S(2)}) copy-start(bf16[8,64,256]{2,1,0:T(8,128)(2,1)S(1)} %get-tuple-element.87.refs_2_) | copy-start | bytes 786436 | tf_op jit(solution)/shard_map/cond
  74.0 22.3 %collective-permute-start.1 = (bf16[8,64,256]{2,1,0:T(8,128)(2,1)S(1)}, bf16[8,64,256]{2,1,0:T(8,128)(2,1)S(1)}, u32[]{:S(2)}, u32[]{:S(2)}) collective-permute-start(bf16[8,64,256]{2,1,0:T(8,128)(2,1)S(1)} %get-tuple-element.87.refs_2_), channel_id=1, source_target_pairs={{1,0},{2,1},{3,2},{4,3},{5,4},{6,5},{7,6},{8,7},{9,8},{10,9},{11,1... | collective-permute-start | bytes 786440 | tf_op jit(solution)/shard_map/cond/branch_0_fun/ppermute | solution.py:342
  96.3 0.7 copy-start.8
  100.3 0.8 copy-start.6

commit v4 on v3

--- a/solution.py
+++ b/solution.py
@@ -44,49 +44,78 @@
     return (wide + 0.5 * update).astype(jnp.bfloat16)
 
 
+def project(stream, gain_ref, qkv_ref):
+    features = stream.shape[-1]
+    normed = normalise(stream, gain_ref[...])
+    scale = math.log2(math.e) / math.sqrt(features // HEADS)
+    query = (wide_dot(normed, qkv_ref[:, :features]) * scale).astype(jnp.bfloat16)
+    key = wide_dot(normed, qkv_ref[:, features : 2 * features]).astype(jnp.bfloat16)
+    value = wide_dot(normed, qkv_ref[:, 2 * features :]).astype(jnp.bfloat16)
+    return query, key, value
+
+
+def attend_block(query, key, value, query_marks, key_marks):
+    tokens, features = query.shape
+    size = features // HEADS
+    half = features // 2
+    lane = lax.broadcasted_iota(jnp.int32, (1, features), 1)
+
+    def head_lanes(first):
+        return jnp.where((lane >= first) & (lane < first + size), 1.0, 0.0).astype(jnp.bfloat16)
+
+    results = []
+    for group in range(2):
+        free = features - size if group == 0 else 0
+        keys = key * (1.0 - head_lanes(free)).astype(jnp.bfloat16) + key_marks[group]
+        total = None
+        for h in range(group * HEADS // 2, (group + 1) * HEADS // 2):
+            q = query * head_lanes(h * size) + query_marks[group]
+            scores = lax.dot_general(
+                q, keys, (((1,), (1,)), ((), ())), preferred_element_type=jnp.float32
+            )
+            top = jnp.max(scores, axis=-1, keepdims=True)
+            weights = jnp.exp2(scores - top).astype(jnp.bfloat16)
+            opposite = h * size + (half if group == 0 else -half)
+            v = value * head_lanes(h * size) + head_lanes(opposite)
+            part = wide_dot(weights, v)
+            total = part if total is None else total + part
+        if group == 0:
+            results.append(total[:, :half] / total[:, half:])
+        else:
+            results.append(total[:, half:] / total[:, :half])
+    return jnp.concatenate(results, axis=-1).astype(jnp.bfloat16)
+
+
 def mix_members(x, gain_ref, qkv_ref, out_ref, gain2_ref, in2_ref, out2_ref):
     members, points, features = x.shape
-    tokens = members * points
     size = features // HEADS
-    stream = x.reshape(tokens, features).astype(jnp.float32)
-    normed = normalise(stream, gain_ref[...])
-    query = wide_dot(normed, qkv_ref[:, :features]) * (math.log2(math.e) / math.sqrt(size))
-    key = wide_dot(normed, qkv_ref[:, features : 2 * features]).astype(jnp.bfloat16)
-    value = wide_dot(normed, qkv_ref[:, 2 * features :])
-    query = query.astype(jnp.bfloat16).reshape(members, points, features)
-    key = key.reshape(members, points, features)
-    value = value.astype(jnp.bfloat16).astype(jnp.float32).reshape(members, points, features)
-
-    lane = lax.broadcasted_iota(jnp.int32, (features, 128), 1) % 64
-    head = lax.broadcasted_iota(jnp.int32, (features, 128), 0) // size
-    place = lane - head
-    scores = jnp.zeros((tokens, 128), jnp.float32)
-    for j in range(members):
-        pick = jnp.where((place == j * HEADS) & (lane // HEADS == j), 1.0, 0.0).astype(jnp.bfloat16)
-        product = (query * key[j][None]).reshape(tokens, features)
-        scores = scores + wide_dot(product, pick)
-    top = scores
-    for step in (8, 16, 32):
-        top = jnp.maximum(top, pltpu.roll(top, step, 1))
-    weights = jnp.exp2(scores - top)
-    total = weights
-    for step in (8, 16, 32):
-        total = total + pltpu.roll(total, step, 1)
-    weights = (weights / total).astype(jnp.bfloat16)
-
-    lane = lax.broadcasted_iota(jnp.int32, (128, features), 0)
-    head = lax.broadcasted_iota(jnp.int32, (128, features), 1) // size
-    place = lane - head
-    mixed = None
-    for j in range(members):
-        spread = jnp.where(place == j * HEADS, 1.0, 0.0).astype(jnp.bfloat16)
-        widened = wide_dot(weights, spread).reshape(members, points, features)
-        part = widened * value[j][None]
-        mixed = part if mixed is None else mixed + part
-    mixed = mixed.reshape(tokens, features).astype(jnp.bfloat16)
-    stream = (stream + wide_dot(mixed, out_ref[...])).astype(jnp.bfloat16)
+    blocks = points // size
+    x = x.astype(jnp.float32)
+    stream = jnp.concatenate(
+        [x[:, b * size : (b + 1) * size].reshape(members * size, features) for b in range(blocks)]
+    )
+    query, key, value = project(stream, gain_ref, qkv_ref)
+    tokens = members * size
+    lane = lax.broadcasted_iota(jnp.int32, (tokens, features), 1)
+    point = lax.broadcasted_iota(jnp.int32, (tokens, features), 0) % size
+    query_marks, key_marks = [], []
+    for first in (features - size, 0):
+        same = lane - first == point
+        marked = (lane >= first) & (lane < first + size)
+        query_marks.append(jnp.where(marked & ~same, -FAR, 0.0).astype(jnp.bfloat16))
+        key_marks.append(jnp.where(same, 1.0, 0.0).astype(jnp.bfloat16))
+    attended = []
+    for b in range(blocks):
+        at = slice(b * tokens, (b + 1) * tokens)
+        attended.append(attend_block(query[at], key[at], value[at], query_marks, key_marks))
+    attended = jnp.concatenate(attended)
+    stream = (stream + wide_dot(attended, out_ref[...])).astype(jnp.bfloat16)
     result = feed_forward(stream, gain2_ref, in2_ref, out2_ref)
-    return result.reshape(members, points, features)
+    result = [
+        result[b * tokens : (b + 1) * tokens].reshape(members, size, features)
+        for b in range(blocks)
+    ]
+    return jnp.concatenate(result, axis=1)
 
 
 def first_member_kernel(x_ref, *refs):
@@ -98,11 +127,6 @@
     *params, o_ref = refs
     o_ref[:, 1 - slot] = done_ref[...]
     o_ref[:, slot] = mix_members(x_ref[...], *params)
-
-
-def merging_kernel(first_row, shifts_ref, later_ref, earlier_ref, o_ref):
-    for i in range(o_ref.shape[0]):
-        o_ref[i] = jnp.where(first_row + i >= shifts_ref[0], later_ref[i], earlier_ref[i])
 
 
 def window_kernel(
@@ -124,7 +148,6 @@
     half, longitudes, features = low_ref.shape
     windows = longitudes // WIN
     size = features // HEADS
-    group_lanes = features // 2
     tokens = WIN * WIN
     lat_shift, lon_shift = shifts_ref[0], shifts_ref[1]
     space = lax.axis_index("space")
@@ -158,11 +181,7 @@
             for w in range(windows)
         ]
     )
-    normed = normalise(stream, gain_ref[...])
-    query = wide_dot(normed, qkv_ref[:, :features]) * (math.log2(math.e) / math.sqrt(size))
-    query = query.astype(jnp.bfloat16)
-    key = wide_dot(normed, qkv_ref[:, features : 2 * features])
-    value = wide_dot(normed, qkv_ref[:, 2 * features :]).astype(jnp.bfloat16)
+    query, key, value = project(stream, gain_ref, qkv_ref)
 
     for copy in copies:
         copy.wait()
@@ -173,13 +192,6 @@
     kind_lane = lax.broadcasted_iota(jnp.int32, (WIN, WIN, longitudes), 2)
 
     lane = lax.broadcasted_iota(jnp.int32, (tokens, features), 1)
-    lane_row = lax.broadcasted_iota(jnp.int32, (1, features), 1)
-
-    def head_lanes(first):
-        return jnp.where(
-            (lane_row >= first) & (lane_row < first + size), 1.0, 0.0
-        ).astype(jnp.bfloat16)
-
     attended = []
     for w in range(windows):
         at = slice(w * tokens, (w + 1) * tokens)
@@ -188,32 +200,18 @@
         )
         kind = jnp.where(kind_lane == wanted, kinds, 0.0).reshape(tokens, longitudes)
         kind = jnp.sum(kind, axis=-1, keepdims=True)
-        halves = []
-        for group in range(2):
-            first = features - size if group == 0 else 0
-            query_marks = jnp.where(
-                lane == first, -FAR * kind, jnp.where(lane == first + 1, -FAR * (1.0 - kind), 0.0)
-            ).astype(jnp.bfloat16)
-            marked = jnp.where(lane == first, 1.0 - kind, jnp.where(lane == first + 1, kind, 0.0))
-            free = (lane >= first) & (lane < first + size)
-            keys = jnp.where(free, marked, key[at]).astype(jnp.bfloat16)
-            total = None
-            for h in range(group * HEADS // 2, (group + 1) * HEADS // 2):
-                q = query[at] * head_lanes(h * size) + query_marks
-                scores = lax.dot_general(
-                    q, keys, (((1,), (1,)), ((), ())), preferred_element_type=jnp.float32
-                )
-                top = jnp.max(scores, axis=-1, keepdims=True)
-                weights = jnp.exp2(scores - top).astype(jnp.bfloat16)
-                opposite = h * size + (group_lanes if group == 0 else -group_lanes)
-                v = value[at] * head_lanes(h * size) + head_lanes(opposite)
-                part = wide_dot(weights, v)
-                total = part if total is None else total + part
-            if group == 0:
-                halves.append(total[:, :group_lanes] / total[:, group_lanes:])
-            else:
-                halves.append(total[:, group_lanes:] / total[:, :group_lanes])
-        attended.append(jnp.concatenate(halves, axis=-1).astype(jnp.bfloat16))
+        query_marks, key_marks = [], []
+        for first in (features - size, 0):
+            here, following = lane == first, lane == first + 1
+            query_marks.append(
+                jnp.where(
+                    here, -FAR * kind, jnp.where(following, -FAR * (1.0 - kind), 0.0)
+                ).astype(jnp.bfloat16)
+            )
+            key_marks.append(
+                jnp.where(here, 1.0 - kind, jnp.where(following, kind, 0.0)).astype(jnp.bfloat16)
+            )
+        attended.append(attend_block(query[at], key[at], value[at], query_marks, key_marks))
     attended = jnp.concatenate(attended)
     stream = (stream + wide_dot(attended, out_ref[...])).astype(jnp.bfloat16)
     result = feed_forward(stream, gain2_ref, in2_ref, out2_ref).astype(jnp.float32)
@@ -259,18 +257,6 @@
         compiler_params=LARGE,
         cost_estimate=cost(512, 1600000),
     )(points, done, *params)
-
-
-def merge_rows(first_row, shifts, later, earlier):
-    def kernel(*refs):
-        merging_kernel(first_row, *refs)
-
-    return pl.pallas_call(
-        kernel,
-        out_shape=jax.ShapeDtypeStruct(later.shape, jnp.bfloat16),
-        in_specs=[SMEM, VMEM, VMEM],
-        out_specs=VMEM,
-    )(shifts, later, earlier)
 
 
 def window_layer(window_below, shifts, region, kinds, *params):
@@ -322,25 +308,47 @@
     def exchange(parts):
         return lax.all_to_all(parts, "member", split_axis=0, concat_axis=0, tiled=True)
 
+    row = jnp.arange(rows, dtype=jnp.int32)[:, None, None]
+    lacking = jnp.minimum(shifts[0], rows - shifts[0])
+    steps = [0, 2, 4, 6, 8]
+    step = (lacking + 1) // 2
+
+    def passed(array, count, pairs, at_start):
+        if count == 0:
+            return jnp.zeros_like(array)
+        sent = array[:count] if at_start else array[half - count :]
+        received = lax.ppermute(sent, "space", pairs)
+        rest = jnp.zeros((half - count, longitudes, features), array.dtype)
+        return jnp.concatenate([received, rest] if at_start else [rest, received])
+
     def run(window_below):
-        low, high = lax.optimization_barrier((ensemble[0, :half], ensemble[0, half:]))
+        ahead, back = (down, up) if window_below else (up, down)
+        late = row[:half] >= shifts[0] if window_below else row[half:] >= shifts[0]
+        low, high = ensemble[0, :half], ensemble[0, half:]
         settled, open_half = (high, low) if window_below else (low, high)
-        other = lax.ppermute(open_half, "space", down if window_below else up)
-        first = exchange(settled)
-        if window_below:
-            merged = merge_rows(0, shifts, open_half, other)
-        else:
-            merged = merge_rows(half, shifts, other, open_half)
+
+        def begin(count):
+            other = passed(open_half, count, ahead, window_below)
+            first = exchange(settled)
+            pair = (open_half, other) if window_below else (other, open_half)
+            return first, jnp.where(late, *pair)
+
+        def end(count, result):
+            other = passed(result, count, back, window_below)
+            pair = (result, other) if window_below else (other, result)
+            return jnp.where(late, *pair)
+
+        first, merged = lax.switch(step, [lambda n=n: begin(n) for n in steps])
         second = exchange(merged)
         first = first_member_layer(first, *members_first)
         mixed = second_member_layer(0 if window_below else 1, second, first, *members_first)
         region = exchange(mixed)
         low, high = window_layer(window_below, shifts, region, land_sea, *windows_second)
         if window_below:
-            back = lax.ppermute(low, "space", up)
-            return jnp.concatenate([merge_rows(0, shifts, low, back), high])
-        back = lax.ppermute(high, "space", down)
-        return jnp.concatenate([low, merge_rows(half, shifts, back, high)])
+            low = lax.switch(step, [lambda n=n: end(n, low) for n in steps])
+        else:
+            high = lax.switch(step, [lambda n=n: end(n, high) for n in steps])
+        return jnp.concatenate([low, high])
 
     out = lax.cond(shifts[0] <= half, lambda: run(True), lambda: run(False))
     return out[None]

time: 102 us -> 105 us (1.029)
  the two profiles are of different devices: /device:TPU:30 before, /device:TPU:1 now
where the time goes in v4:
time: 105 us; the launch traced here: 104 us
  waiting for transfers between devices  41 us (39%)
  starting transfers between devices  31 us (30%)
  Pallas kernels  14.7 us (14%)
  loops' own time  8.08 us (8%)
  local copies, waits for them, and re-layouts  5.5 us (5%)
  other arithmetic  2.97 us (3%)
    ppermute x2, waiting for transfers between devices, passed(): received = lax.ppermute(sent, 'space', pairs)  22.2 us
    all_to_all x3, starting transfers between devices, exchange(): lax.all_to_all(parts, 'member', split_axis=0, concat_axis=0, tiled=True)  21.2 us
    all_to_all x3, waiting for transfers between devices, exchange(): lax.all_to_all(parts, 'member', split_axis=0, concat_axis=0, tiled=True)  18.8 us
    ppermute x2, starting transfers between devices, passed(): received = lax.ppermute(sent, 'space', pairs)  9.74 us
    another operation x1, loops' own time, on_device(): out = lax.cond(shifts[0] <= half, lambda: run(True), lambda: run(False))  7.98 us
    pallas_call x1, Pallas kernels, window_layer(): pl.pallas_call(kernel, out_shape=[jax.ShapeDtypeStruct((half, longitudes,...  6.48 us
    pallas_call x1, Pallas kernels, first_member_layer(): pl.pallas_call(first_member_kernel, out_shape=jax.ShapeDtypeStruct(points...  4.19 us
    pallas_call x1, Pallas kernels, second_member_layer(): pl.pallas_call(kernel, out_shape=jax.ShapeDtypeStruct((members, 2, *rest)...  4.03 us
  transfers between devices with their start and end apart: 5, of which 4 were waited for; matrix products, arithmetic and copies ran while one was open for 1% of the time, Pallas kernels for 4%

profile of v4, /device:TPU:1, one launch (start us, length us, event | category | flops | bytes accessed | tf_op | source)
XLA Modules:
  0.0 103.9 jit_solution(7702288607051412000)
XLA Ops:
  0.0 0.0 copy-start.23
  0.0 0.7 copy-done.23
  0.7 0.0 copy-start.22
  0.8 0.0 copy-start.20
  0.8 0.0 copy-start.21
  0.8 0.0 copy-start.19
  0.8 0.6 copy-done.22
  1.4 0.0 copy-done.20
  1.5 0.0 copy-done.21
  1.5 0.0 copy-done.19
  1.5 101.1 %conditional.5 = (bf16[1,16,64,256]{3,2,1,0:T(8,128)(2,1)S(1)}) conditional(s32[]{:T(128)} %convert_element_type.3, (s32[]{:T(128)}, pred[]{:T(512)}, bf16[1,16,64,256]{3,2,1,0:T(8,128)(2,1)}, s32[16,1,1]{0,2,1:T(1,128)S(1)}, s32[2]{0:T(128)S(1)}, /*index=5*/f32[256]{0:T(256)S(1)}, f32[256]{0:T(256)S(1)}, bf16[256,768]{1,0:T(8,128)(2,1)}, ...), branch_computations={%region_0.11_spmd, %region_11.22_spmd} | conditional | flops 3686924288 | bytes 32899890 | solution.py:353
  9.1 1.8 %slice_bitcast_fusion.2 = (bf16[8,64,256]{2,1,0:T(8,128)(2,1)S(1)}, bf16[8,64,256]{2,1,0:T(8,128)(2,1)}) fusion(bf16[1,16,64,256]{3,2,1,0:T(8,128)(2,1)} %get-tuple-element.339), kind=kLoop, calls=%fused_computation.7 | loop fusion | bytes 1048576 | tf_op jit(solution)/shard_map/cond/branch_1_fun/squeeze | solution.py:327
  10.9 0.0 copy-start.12
  10.9 22.3 %conditional.2 = (bf16[8,64,256]{2,1,0:T(8,128)(2,1)}, bf16[8,64,256]{2,1,0:T(8,128)(2,1)S(1)}, bf16[8,64,256]{2,1,0:T(8,128)(2,1)}, pred[8,1,1]{0,2,1:T(4,128)(4,1)S(1)}) conditional(s32[]{:T(128)} %clamp.5, (bf16[8,64,256]{2,1,0:T(8,128)(2,1)}, bf16[8,64,256]{2,1,0:T(8,128)(2,1)S(1)}, ...), branch_computations={%region_12.12_spmd, %region_13.13_spmd, %region_14.14_spmd, %regio... | conditional | bytes 2424938 | solution.py:341
  10.9 7.5 %all-to-all-start.8 = ((bf16[8,64,256]{2,1,0:T(8,128)(2,1)}), bf16[8,64,256]{2,1,0:T(8,128)(2,1)}, u32[]{:S(2)}, u32[]{:S(2)}) async-start(bf16[8,64,256]{2,1,0:T(8,128)(2,1)} %get-tuple-element.320), calls=%async_computation.8 | async-start | bytes 524288 | tf_op jit(solution)/shard_map/cond/branch_1_fun/cond/branch_3_fun/all_to_all | solution.py:309
  18.5 9.7 %collective-permute-start.10 = (bf16[6,64,256]{2,1,0:T(8,128)(2,1)S(1)}, bf16[6,64,256]{2,1,0:T(8,128)(2,1)S(1)}, u32[]{:S(2)}, u32[]{:S(2)}) collective-permute-start(bf16[6,64,256]{2,1,0:T(8,128)(2,1)S(1)} %slice.56), channel_id=1, source_target_pairs={{1,0},{2,1},{3,2},{4,3},{5,4},{6,5},{7,6},{8,7},{9,8},{10,9},{11,1... | collective-permute-start | bytes 589832 | tf_op jit(solution)/shard_map/cond/branch_1_fun/cond/branch_3_fun/ppermute | solution.py:320
  28.2 4.3 %collective-permute-done.10 = bf16[6,64,256]{2,1,0:T(8,128)(2,1)S(1)} collective-permute-done((bf16[6,64,256]{2,1,0:T(8,128)(2,1)S(1)}, bf16[6,64,256]{2,1,0:T(8,128)(2,1)S(1)}, u32[]{:S(2)}, u32[]{:S(2)}) %collective-permute-start.10) | collective-permute-done | bytes 196640 | tf_op jit(solution)/shard_map/cond/branch_1_fun/cond/branch_3_fun/ppermute | solution.py:320
  32.4 0.7 concatenate.37
  33.2 0.0 all-to-all-done.8
  33.2 0.0 copy-start.6
  33.2 1.8 %broadcast_select_fusion.3 = bf16[8,64,256]{2,1,0:T(8,128)(2,1)} fusion(bf16[8,64,256]{2,1,0:T(8,128)(2,1)S(1)} %get-tuple-element.342, bf16[8,64,256]{2,1,0:T(8,128)(2,1)} %get-tuple-element.343, pred[8]{0:T(512)(128)(4,1)S(1)} %bitcast.32), kind=kLoop, calls=%fused_computation.10 | loop fusion | flops 131072 | bytes 786440 | tf_op jit(solution)/shard_map/cond/branch_1_fun/cond/branch_0_fun/jit(_where)/select_n | solution.py:334
  35.0 0.0 copy-start.16
  35.0 8.8 %all-to-all-start.12 = ((bf16[8,64,256]{2,1,0:T(8,128)(2,1)}), bf16[8,64,256]{2,1,0:T(8,128)(2,1)S(1)}, u32[]{:S(2)}, u32[]{:S(2)}) async-start(bf16[8,64,256]{2,1,0:T(8,128)(2,1)} %broadcast_select_fusion.3), calls=%async_computation.12 | async-start | bytes 524288 | tf_op jit(solution)/shard_map/cond/branch_1_fun/all_to_all | solution.py:309
  43.8 0.0 copy-done.12
  43.8 0.0 copy-done.4
  43.8 0.0 copy-done.6
  43.8 0.0 copy-done.16
  43.9 4.2 %branch_1_fun.3.refs_1_ = bf16[8,64,256]{2,1,0:T(8,128)(2,1)S(1)} custom-call(bf16[8,64,256]{2,1,0:T(8,128)(2,1)} %get-tuple-element.344.x_ref, f32[1,256]{1,0:T(1,128)S(1)} %bitcast.36, bf16[256,768]{1,0:T(8,128)(2,1)S(1)} %copy-done.12, bf16[256,256]{1,0:T(8,128)(2,1)S(1)} %copy-done.16, f32[1,256]{1,0:T(1,128)S(1)} %bitcast.40, ...), custom_call_target="tpu_custom_call" | custom-call | flops 819200000 | bytes 3145728 | tf_op jit(solution)/shard_map/cond/branch_1_fun/pallas_call | solution.py:236
  48.0 4.5 %all-to-all-done.12.refs_0_ = bf16[8,64,256]{2,1,0:T(8,128)(2,1)S(1)} async-done(((bf16[8,64,256]{2,1,0:T(8,128)(2,1)}), bf16[8,64,256]{2,1,0:T(8,128)(2,1)S(1)}, u32[]{:S(2)}, u32[]{:S(2)}) %all-to-all-start.12) | async-done | bytes 262176 | tf_op jit(solution)/shard_map/cond/branch_1_fun/all_to_all | solution.py:309
  52.5 0.0 copy-start.14
  52.5 4.0 %branch_1_fun.4 = bf16[8,2,64,256]{3,2,1,0:T(8,128)(2,1)} custom-call(bf16[8,64,256]{2,1,0:T(8,128)(2,1)S(1)} %all-to-all-done.12.refs_0_, bf16[8,64,256]{2,1,0:T(8,128)(2,1)S(1)} %branch_1_fun.3.refs_1_, f32[1,256]{1,0:T(1,128)S(1)} %bitcast.37, bf16[256,768]{1,0:T(8,128)(2,1)S(1)} %copy-done.12, bf16[256,256]{1,0:T(8,128)(2,1)S(1)} %copy-done.16, ...), custom_call_target="tpu_custom_call" | custom-call | flops 819200000 | bytes 3145728 | tf_op jit(solution)/shard_map/cond/branch_1_fun/pallas_call | solution.py:252
  56.6 4.8 %all-to-all-start.13 = ((bf16[8,2,64,256]{3,2,1,0:T(8,128)(2,1)}), bf16[8,2,64,256]{3,2,1,0:T(8,128)(2,1)S(1)}, u32[]{:S(2)}, u32[]{:S(2)}) async-start(bf16[8,2,64,256]{3,2,1,0:T(8,128)(2,1)} %branch_1_fun.4), calls=%async_computation.13 | async-start | bytes 1048576 | tf_op jit(solution)/shard_map/cond/branch_1_fun/all_to_all | solution.py:309
  61.4 0.0 copy-done.1
  61.4 0.0 copy-start.18
  61.5 0.1 copy.19.refs_2_
  61.6 14.3 %all-to-all-done.13.refs_1_ = bf16[8,2,64,256]{3,2,1,0:T(8,128)(2,1)S(1)} async-done(((bf16[8,2,64,256]{3,2,1,0:T(8,128)(2,1)}), bf16[8,2,64,256]{3,2,1,0:T(8,128)(2,1)S(1)}, u32[]{:S(2)}, u32[]{:S(2)}) %all-to-all-start.13) | async-done | bytes 524320 | tf_op jit(solution)/shard_map/cond/branch_1_fun/all_to_all | solution.py:309
  75.9 0.0 copy-done.14
  75.9 0.0 copy-done.8
  75.9 0.0 copy-done.10
  75.9 0.0 copy-done.18
  75.9 6.5 %branch_1_fun.5 = (bf16[8,64,256]{2,1,0:T(8,128)(2,1)S(1)}, bf16[8,64,256]{2,1,0:T(8,128)(2,1)S(1)}) custom-call(s32[2]{0:T(128)S(1)} %get-tuple-element.338.refs_0_, bf16[8,2,64,256]{3,2,1,0:T(8,128)(2,1)S(1)} %all-to-all-done.13.refs_1_, s32[512,64]{1,0:T(8,128)S(1)} %copy.19.refs_2_, f32[1,256]{1,0:T(1,128)S(1)} %bitcast.43, ...), custom_call_target="tpu_custom_call" | custom-call | flops 2048000000 | bytes 3145728 | tf_op jit(solution)/shard_map/cond/branch_1_fun/pallas_call | solution.py:268
  82.4 18.8 %conditional.3 = (bf16[8,64,256]{2,1,0:T(8,128)(2,1)S(1)}, bf16[8,64,256]{2,1,0:T(8,128)(2,1)}, pred[8,1,1]{0,2,1:T(4,128)(4,1)S(1)}) conditional(s32[]{:T(128)} %clamp.5, (bf16[8,64,256]{2,1,0:T(8,128)(2,1)S(1)}, pred[8,1,1]{0,2,1:T(4,128)(4,1)S(1)}) %tuple.160, (bf16[8,64,256]{2,1,0:T(8,128)(2,1)S(1)}, ...), branch_computations={%region_17.17_spmd, %region_18.18_spmd, %region_19.19_spmd, %regio... | conditional | bytes 1638466 | solution.py:348
  82.5 0.1 collective-permute-start.14
  82.6 17.9 %collective-permute-done.14 = bf16[6,64,256]{2,1,0:T(8,128)(2,1)S(1)} collective-permute-done((bf16[6,64,256]{2,1,0:T(8,128)(2,1)S(1)}, bf16[6,64,256]{2,1,0:T(8,128)(2,1)S(1)}, u32[]{:S(2)}, u32[]{:S(2)}) %collective-permute-start.14) | collective-permute-done | bytes 196640 | tf_op jit(solution)/shard_map/cond/branch_1_fun/cond/branch_3_fun/ppermute | solution.py:320
  100.5 0.7 concatenate.40
  101.2 1.0 %broadcast_select_fusion.2 = bf16[8,64,256]{2,1,0:T(8,128)(2,1)S(1)} fusion(bf16[8,64,256]{2,1,0:T(8,128)(2,1)S(1)} %get-tuple-element.360, bf16[8,64,256]{2,1,0:T(8,128)(2,1)} %get-tuple-element.361, pred[8]{0:T(512)(128)(4,1)S(1)} %bitcast.33), kind=kLoop, calls=%fused_computation.9 | loop fusion | flops 131072 | bytes 786440 | tf_op jit(solution)/shard_map/cond/branch_1_fun/cond/branch_0_fun/jit(_where)/select_n | solution.py:339
  102.6 0.0 copy-start.2
  102.6 0.8 copy-done.2
  (10 shorter events, 0.1 us)
Async XLA Ops:
  0.0 0.7 copy-start.23
  0.7 0.7 copy-start.22
  0.8 0.7 copy-start.20
  0.8 0.7 copy-start.21
  0.8 0.7 copy-start.19
  10.9 32.9 %copy-start.12 = (bf16[256,768]{1,0:T(8,128)(2,1)S(1)}, bf16[256,768]{1,0:T(8,128)(2,1)}, u32[]{:S(2)}) copy-start(bf16[256,768]{1,0:T(8,128)(2,1)} %get-tuple-element.346.refs_1_.refs_3_) | copy-start | bytes 1179652 | tf_op jit(solution)/shard_map/cond
  10.9 22.2 %all-to-all-start.8 = ((bf16[8,64,256]{2,1,0:T(8,128)(2,1)}), bf16[8,64,256]{2,1,0:T(8,128)(2,1)}, u32[]{:S(2)}, u32[]{:S(2)}) async-start(bf16[8,64,256]{2,1,0:T(8,128)(2,1)} %get-tuple-element.320), calls=%async_computation.8 | async-start | bytes 524288 | tf_op jit(solution)/shard_map/cond/branch_1_fun/cond/branch_3_fun/all_to_all | solution.py:309
  18.5 13.9 %collective-permute-start.10 = (bf16[6,64,256]{2,1,0:T(8,128)(2,1)S(1)}, bf16[6,64,256]{2,1,0:T(8,128)(2,1)S(1)}, u32[]{:S(2)}, u32[]{:S(2)}) collective-permute-start(bf16[6,64,256]{2,1,0:T(8,128)(2,1)S(1)} %slice.56), channel_id=1, source_target_pairs={{1,0},{2,1},{3,2},{4,3},{5,4},{6,5},{7,6},{8,7},{9,8},{10,9},{11,1... | collective-permute-start | bytes 589832 | tf_op jit(solution)/shard_map/cond/branch_1_fun/cond/branch_3_fun/ppermute | solution.py:320
  33.2 10.7 %copy-start.4 = (bf16[256,1024]{1,0:T(8,128)(2,1)S(1)}, bf16[256,1024]{1,0:T(8,128)(2,1)}, u32[]{:S(2)}) copy-start(bf16[256,1024]{1,0:T(8,128)(2,1)} %get-tuple-element.349.refs_4_.refs_6_) | copy-start | bytes 1572868 | tf_op jit(solution)/shard_map/cond
  33.2 10.7 %copy-start.6 = (bf16[1024,256]{1,0:T(8,128)(2,1)S(1)}, bf16[1024,256]{1,0:T(8,128)(2,1)}, u32[]{:S(2)}) copy-start(bf16[1024,256]{1,0:T(8,128)(2,1)} %get-tuple-element.350.refs_5_.refs_7_) | copy-start | bytes 1572868 | tf_op jit(solution)/shard_map/cond
  35.0 8.8 %copy-start.16 = (bf16[256,256]{1,0:T(8,128)(2,1)S(1)}, bf16[256,256]{1,0:T(8,128)(2,1)}, u32[]{:S(2)}) copy-start(bf16[256,256]{1,0:T(8,128)(2,1)} %get-tuple-element.347.refs_2_.refs_4_) | copy-start | bytes 393220 | tf_op jit(solution)/shard_map/cond
  35.0 17.5 %all-to-all-start.12 = ((bf16[8,64,256]{2,1,0:T(8,128)(2,1)}), bf16[8,64,256]{2,1,0:T(8,128)(2,1)S(1)}, u32[]{:S(2)}, u32[]{:S(2)}) async-start(bf16[8,64,256]{2,1,0:T(8,128)(2,1)} %broadcast_select_fusion.3), calls=%async_computation.12 | async-start | bytes 524288 | tf_op jit(solution)/shard_map/cond/branch_1_fun/all_to_all | solution.py:309
  52.5 23.4 %copy-start.14 = (bf16[256,768]{1,0:T(8,128)(2,1)S(1)}, bf16[256,768]{1,0:T(8,128)(2,1)}, u32[]{:S(2)}) copy-start(bf16[256,768]{1,0:T(8,128)(2,1)} %get-tuple-element.353.refs_4_) | copy-start | bytes 1179652 | tf_op jit(solution)/shard_map/cond
  56.6 4.9 %copy-start.1 = (s32[512,64]{0,1:T(8,128)S(1)}, s32[512,64]{0,1:T(8,128)}, u32[]{:S(2)}) copy-start(s32[512,64]{0,1:T(8,128)} %get-tuple-element.395) | copy-start | bytes 393220 | tf_op jit(solution)/shard_map/cond
  56.6 19.3 %copy-start.8 = (bf16[256,1024]{1,0:T(8,128)(2,1)S(1)}, bf16[256,1024]{1,0:T(8,128)(2,1)}, u32[]{:S(2)}) copy-start(bf16[256,1024]{1,0:T(8,128)(2,1)} %get-tuple-element.356.refs_7_) | copy-start | bytes 1572868 | tf_op jit(solution)/shard_map/cond
  56.6 19.3 %copy-start.10 = (bf16[1024,256]{1,0:T(8,128)(2,1)S(1)}, bf16[1024,256]{1,0:T(8,128)(2,1)}, u32[]{:S(2)}) copy-start(bf16[1024,256]{1,0:T(8,128)(2,1)} %get-tuple-element.357.refs_8_) | copy-start | bytes 1572868 | tf_op jit(solution)/shard_map/cond
  56.6 19.3 %all-to-all-start.13 = ((bf16[8,2,64,256]{3,2,1,0:T(8,128)(2,1)}), bf16[8,2,64,256]{3,2,1,0:T(8,128)(2,1)S(1)}, u32[]{:S(2)}, u32[]{:S(2)}) async-start(bf16[8,2,64,256]{3,2,1,0:T(8,128)(2,1)} %branch_1_fun.4), calls=%async_computation.13 | async-start | bytes 1048576 | tf_op jit(solution)/shard_map/cond/branch_1_fun/all_to_all | solution.py:309
  61.4 14.5 %copy-start.18 = (bf16[256,256]{1,0:T(8,128)(2,1)S(1)}, bf16[256,256]{1,0:T(8,128)(2,1)}, u32[]{:S(2)}) copy-start(bf16[256,256]{1,0:T(8,128)(2,1)} %get-tuple-element.354.refs_5_) | copy-start | bytes 393220 | tf_op jit(solution)/shard_map/cond
  82.5 18.0 %collective-permute-start.14 = (bf16[6,64,256]{2,1,0:T(8,128)(2,1)S(1)}, bf16[6,64,256]{2,1,0:T(8,128)(2,1)S(1)}, u32[]{:S(2)}, u32[]{:S(2)}) collective-permute-start(bf16[6,64,256]{2,1,0:T(8,128)(2,1)S(1)} %slice.59), channel_id=1, source_target_pairs={{0,1},{1,2},{2,3},{3,4},{4,5},{5,6},{6,7},{7,8},{8,9},{9,10},{10,1... | collective-permute-start | bytes 589832 | tf_op jit(solution)/shard_map/cond/branch_1_fun/cond/branch_3_fun/ppermute | solution.py:320
  102.6 0.8 copy-start.2
